TPU v7x, 128 devices: a whole 4x4x4 slice. The times are simulated.
128 devices in a mesh: gx: 16 (over y, z), gy: 8 (over x, core).
Axes of the slice: x: 4, y: 4, z: 4, core: 2. Of those that a mesh axis runs over, the one named last changes fastest.
Arguments:
- raw: bfloat16 [8, 128, 1024], P('gy', None, 'gx'), may hold values from -6 to 6
- section_order: int32 [8], replicated, may hold values from 0 to 7, each once
- margins: int32 [16, 8], replicated, may hold values from 1 to 4, as said below
- w_in: bfloat16 [28, 9], replicated, may hold values from -2 to 2
- b_in: float32 [28], replicated, may hold values from -3 to 3
- w_a: bfloat16 [27, 28, 28], replicated, may hold values from -0.21875 to 0.21875
- b_a: float32 [28], replicated, may hold values from -3 to 3
- w_d: bfloat16 [9, 36, 28], replicated, may hold values from -0.375 to 0.375
- b_d: float32 [36], replicated, may hold values from -3 to 3
- w_u: bfloat16 [28, 36], replicated, may hold values from -1 to 1
- w_o: bfloat16 [3, 28], replicated, may hold values from -1 to 1
- b_o: float32 [3], replicated, may hold values from -3 to 3
Outputs:
- affinities: float32 [3, 8, 128, 1024], P(None, None, 'gx', 'gy')
Inputs may be any that keep to these rules, and one draw needn't show every extreme that they name: `section_order`: each section is named once. margins of the groups; one group has margin 4 in every draw.
All inputs are finite; a program needn't handle non-finite values.
Results may differ from a plain program's by a relative error of at most 0.0065.
Values may be sent and summed in bfloat16 or wider, within the bound.
A program may use at most 128 MiB of HBM per device.

v0:
```python
import functools

import jax
import jax.numpy as jnp
from jax import lax
from jax.experimental import pallas as pl
from jax.experimental.pallas import tpu as pltpu
from jax.sharding import PartitionSpec as P

MESH = pl.DeviceIdType.MESH
F32 = jnp.float32
BF16 = jnp.bfloat16
BIG = -1e30

LEFT_AT = 96
RIGHT_AT = 32 - 127


def iota(shape, dim):
    return lax.broadcasted_iota(jnp.int32, shape, dim)


def within(x, low, high):
    return (x >= low) & (x <= high)


def dot(a, b):
    return jnp.dot(a, b, preferred_element_type=F32)


def neighbours(gi):
    odd = lax.rem(gi, 2)
    column = lax.div(gi, 2)
    beside = lax.rem(column + 7 + 2 * odd, 8)
    return odd, column, beside


def exchange_kernel(raw_ref, got_ref, send_ref, send_sem, recv_sem):
    gi = lax.axis_index("gx")
    gj = lax.axis_index("gy")
    odd, column, beside = neighbours(gi)
    barrier = pltpu.get_barrier_semaphore()

    def greet(n, carry):
        strip = lax.rem(2 * gj + 15 + lax.rem(n, 4), 16)
        slab = lax.div(n, 4)

        @pl.when((strip != gi) | (slab != gj))
        def _():
            pl.semaphore_signal(barrier, inc=1, device_id=(strip, slab), device_id_type=MESH)

        return carry

    lax.fori_loop(0, 32, greet, 0)

    row = iota((256, 128), 0)
    rows = (iota((256, 128), 1) == 8 * (row // 16) - 4 + row % 16).astype(F32).astype(BF16)
    lane = iota((64, 256), 1)
    tile = lane % 128
    even_main = jnp.where(tile < 64, tile, jnp.where(within(tile, 96, 100), tile - LEFT_AT, -1))
    odd_main = jnp.where(tile >= 64, tile - 64, jnp.where(within(tile, 28, 32), tile + 31, -1))
    even_side = jnp.where(tile < 4, tile, jnp.where(within(tile, 33, 36), tile - 33, -1))
    odd_side = jnp.where(tile >= 124, tile - 64, jnp.where(within(tile, 92, 95), tile - 32, -1))
    ends = (gi == 0) | (gi == 15)
    main = jnp.where(odd == 1, odd_main, even_main)
    side = jnp.where(ends, -1, jnp.where(odd == 1, odd_side, even_side))
    cols = (iota((64, 256), 0) == jnp.where(lane < 128, main, side)).astype(F32).astype(BF16)
    picked = dot(rows, raw_ref[0]).astype(BF16)
    message = dot(picked, cols).astype(BF16)
    send_ref[0:16] = message[:, 0:128].reshape(16, 16, 128)
    send_ref[16:32] = message[:, 128:256].reshape(16, 16, 128)

    at_home = (gj == column) | (gj == beside)

    @pl.when(at_home)
    def _():
        pl.semaphore_wait(barrier, 31)

    @pl.when(jnp.logical_not(at_home))
    def _():
        pl.semaphore_wait(barrier, 32)

    def send(n, carry):
        target = lax.rem(gi + n, 16)
        for kind in range(2):
            where_to = column if kind == 0 else beside
            slot = odd if kind == 0 else 3 - odd
            source = send_ref.at[target + 16 * kind]
            place = got_ref.at[slot, gj]
            here = (target == gi) & (where_to == gj)

            @pl.when(here)
            def _():
                pltpu.make_async_copy(source, place, recv_sem).start()

            @pl.when(jnp.logical_not(here))
            def _():
                pltpu.make_async_remote_copy(
                    src_ref=source,
                    dst_ref=place,
                    send_sem=send_sem,
                    recv_sem=recv_sem,
                    device_id=(target, where_to),
                    device_id_type=MESH,
                ).start()

        return carry

    lax.fori_loop(0, 16, send, 0)
    pltpu.make_async_copy(got_ref, got_ref, recv_sem).wait()

    @pl.when(at_home)
    def _():
        pltpu.make_async_copy(send_ref.at[0:31], send_ref.at[0:31], send_sem).wait()

    @pl.when(jnp.logical_not(at_home))
    def _():
        pltpu.make_async_copy(send_ref, send_ref, send_sem).wait()


def exchange(raw):
    return pl.pallas_call(
        exchange_kernel,
        out_shape=jax.ShapeDtypeStruct((4, 8, 16, 128), BF16),
        in_specs=[pl.BlockSpec(memory_space=pltpu.VMEM)],
        out_specs=pl.BlockSpec(memory_space=pl.ANY),
        scratch_shapes=[
            pltpu.VMEM((32, 16, 128), BF16),
            pltpu.SemaphoreType.DMA,
            pltpu.SemaphoreType.DMA,
        ],
        compiler_params=pltpu.CompilerParams(collective_id=0, has_side_effects=True),
    )(raw)


def as_column(row, size):
    shape = (size, row.shape[1])
    return jnp.sum(jnp.where(iota(shape, 0) == iota(shape, 1), row, 0.0), axis=1, keepdims=True)


def split(x):
    high = x.astype(BF16)
    return high, (x - high.astype(F32)).astype(BF16)


def fine_lane(coarse):
    return jnp.where(
        coarse <= 64,
        2 * coarse,
        jnp.where(
            within(coarse, 95, 97),
            2 * coarse + 32,
            jnp.where(within(coarse, 80, 82), 2 * coarse - 3, jnp.where(coarse == 127, 254, -9)),
        ),
    )


def tiled_taps(pad_ref, first, taps, rows, pitch=32):
    tiles = []
    for start in range(0, taps, 128 // pitch):
        tile = None
        for q in range(min(128 // pitch, taps - start)):
            part = pad_ref[first + start + q, 0:rows].astype(F32)
            part = part if q == 0 else pltpu.roll(part, q * pitch, 1)
            tile = part if tile is None else tile + part
        tiles.append(tile)
    return jnp.concatenate(tiles, axis=1)


def network_kernel(
    place,
    order_ref,
    margins_ref,
    b_o_ref,
    got_ref,
    w_in_ref,
    b_in_ref,
    w_a_ref,
    b_a_ref,
    w_d_ref,
    b_d_ref,
    w_u_ref,
    w_o_ref,
    out_ref,
    pad_ref,
    conv_in_ref,
    conv_a_ref,
    conv_d_ref,
    pool_ref,
    spread_ref,
    h_ref,
    a_ref,
    cut_ref,
    d_ref,
    e_ref,
):
    gi, gj = place()

    pad_ref[...] = jnp.zeros_like(pad_ref)
    pad_ref[0:27, 0:28, 0:28] = w_a_ref[...]
    for dz in range(3):
        taps = tiled_taps(pad_ref, 9 * dz, 9, 32)
        lane = iota((32, 384), 1)
        later = pltpu.roll(taps, 96, 1)
        at = 32 * dz
        conv_a_ref[at : at + 32] = jnp.where(lane < 288, later, 0.0).astype(BF16)
        conv_a_ref[96 + at : 128 + at] = taps.astype(BF16)
        conv_a_ref[192 + at : 224 + at] = later.astype(BF16)
        conv_a_ref[288 + at : 320 + at] = jnp.where(lane >= 96, taps, 0.0).astype(BF16)
    pad_ref[0:9, 0:36, 0:28] = w_d_ref[...]
    taps = tiled_taps(pad_ref, 0, 9, 48)
    conv_d_ref[0] = taps.astype(BF16)
    conv_d_ref[1] = pltpu.roll(taps, 384 - 96, 1).astype(BF16)
    bias_a = as_column(b_a_ref[...], 32)
    bias_d = as_column(b_d_ref[...], 48)

    w_in = w_in_ref[...].astype(F32)
    w_in = jnp.concatenate([w_in, jnp.zeros((4, 9), F32)], axis=0)
    lane = iota((32, 128), 1)
    base = jnp.zeros((32, 128), F32)
    for dy in range(3):
        for dx in range(3):
            tap = dy * 3 + dx
            base = base + jnp.where(lane == 16 * dx + dy, w_in[:, tap : tap + 1], 0.0)
    bias = as_column(b_in_ref[...], 32)
    rest = bias
    extra = jnp.where(lane == 51, BIG, 0.0)
    for n in range(3):
        part = rest.astype(BF16).astype(F32)
        extra = extra + jnp.where(lane == 48 + n, part, 0.0)
        rest = rest - part
    for y in range(14):
        taps = extra + (base if y == 0 else pltpu.roll(base, y, 1))
        if y < 3:
            taps = taps + jnp.where(lane == 52, BIG, 0.0)
        if y >= 11:
            taps = taps + jnp.where(lane == 53, BIG, 0.0)
        conv_in_ref[32 * y : 32 * y + 32] = taps.astype(BF16)

    fine = iota((256, 128), 0)
    first = fine_lane(iota((256, 128), 1))
    pool_ref[...] = jnp.where((fine == first) | (fine == first + 1), 0.25, 0.0).astype(BF16)
    fine = iota((128, 256), 1)
    first = fine_lane(iota((128, 256), 0))
    spread = jnp.where((fine == first) | (fine == first + 1), 1.0, 0.0).astype(BF16)
    spread_ref[0:128] = spread
    spread_ref[128:256] = spread

    w_o = w_o_ref[...].astype(F32)
    w_o_rows = jnp.concatenate([jnp.broadcast_to(w_o[o : o + 1], (8, 28)) for o in range(3)], axis=0)
    pad_ref[0] = jnp.zeros((48, 128), BF16)
    pad_ref[0, 0:28, 0:36] = w_u_ref[...]
    w_u = pad_ref[0, 0:32].astype(F32)
    w_u_wide = jnp.concatenate([w_u, jnp.zeros_like(w_u)], axis=1)
    w_u_tiled = w_u_wide
    for n in range(1, 4):
        w_u_tiled = w_u_tiled + pltpu.roll(w_u_wide, 48 * n, 1)
    w_o_pad = jnp.concatenate([w_o_rows, jnp.zeros((24, 4), F32)], axis=1)
    w_q = dot(w_o_pad.astype(BF16), w_u_tiled.astype(BF16))
    y_of = iota((24, 256), 0) % 8
    w_q = jnp.where(iota((24, 256), 1) // 48 == y_of // 2, w_q, 0.0)[:, 0:192]
    w_q_high, w_q_low = split(w_q)
    w_q = jnp.concatenate([w_q_high.astype(F32), w_q_low.astype(F32)], axis=0).astype(BF16)
    w_o_tiled = jnp.concatenate([w_o_pad] * 8, axis=1)
    w_o_diag = jnp.where(iota((24, 256), 1) // 32 == y_of, w_o_tiled, 0.0).astype(BF16)
    row = iota((24, 1), 0)
    bias_o = jnp.where(row < 8, b_o_ref[0], jnp.where(row < 16, b_o_ref[1], b_o_ref[2]))

    def margin(step_y, step_x):
        y, x = gi + step_y, gj + step_x
        inside = (y >= 0) & (y < 16) & (x >= 0) & (x < 8)
        value = margins_ref[jnp.clip(y, 0, 15), jnp.clip(x, 0, 7)]
        return value.astype(F32), jnp.where(inside, 1.0, 0.0)

    def ramp(distance, width):
        return jnp.clip(1.0 - distance / (width + 1.0), 0.0, 1.0)

    y = iota((8, 128), 0)
    lane = iota((8, 128), 1)
    upper = y < 4
    off_y = jnp.where(upper, y + 1, 8 - y).astype(F32)
    leftward = lane >= 64
    from_left = lane - LEFT_AT
    from_right = lane - RIGHT_AT
    is_left = within(from_left, 0, 3)
    is_right = within(from_right, 124, 127)
    off_x = jnp.where(is_left, from_left + 1, jnp.where(is_right, 128 - from_right, 99)).astype(F32)

    def by_place(pairs):
        m = jnp.where(leftward, pairs[0][0], pairs[1][0])
        there = jnp.where(leftward, pairs[0][1], pairs[1][1])
        return m, there

    m_up, in_up = margin(-1, 0)
    m_down, in_down = margin(1, 0)
    weight_y = ramp(off_y, jnp.where(upper, m_up, m_down)) * jnp.where(upper, in_up, in_down)
    m, there = by_place((margin(0, -1), margin(0, 1)))
    weight_x = ramp(off_x, m) * there
    m_top, there_top = by_place((margin(-1, -1), margin(-1, 1)))
    m_low, there_low = by_place((margin(1, -1), margin(1, 1)))
    m = jnp.where(upper, m_top, m_low)
    weight_xy = ramp(off_y, m) * ramp(off_x, m) * jnp.where(upper, there_top, there_low)

    def fold(core, beyond):
        left = jnp.where(lane < 4, pltpu.roll(beyond, 128 - LEFT_AT, 1), 0.0)
        right = jnp.where(lane >= 124, pltpu.roll(beyond, 95, 1), 0.0)
        return core + left + right

    scale = 1.0 / fold(1.0 + weight_y, weight_x + weight_xy)

    column = iota((16, 256), 1)
    kind = iota((16, 256), 0)
    outside = (
        (column == 128 + 100)
        | (column == 128 + 28)
        | (within(column, 252, 255) & (gj == 0))
        | (within(column, 128, 131) & (gj == 7))
    )
    flags = jnp.where(kind < 3, 1.0, 0.0)
    flags = jnp.where((kind == 3) & outside, 1.0, flags)
    flags = jnp.where((kind == 4) & (gi == 0), 1.0, flags)
    flags = jnp.where((kind == 5) & (gi == 15), 1.0, flags)
    tile = iota((16, 128), 1)

    def first_level(z, carry):
        slab = jnp.int32(0)
        for k in range(8):
            slab = slab + jnp.where(order_ref[k] == z, k, 0)
        near, far, before, after = [got_ref[n, slab].astype(F32) for n in range(4)]
        core = jnp.where(tile < 64, near, far)
        low = jnp.where(within(tile, 28, 32), far, after)
        high = jnp.where(within(tile, 96, 100), near, before)
        raw = jnp.concatenate([core, jnp.where(tile < 64, low, high)], axis=1)
        taps = jnp.concatenate([pltpu.roll(raw, 1, 1), raw, pltpu.roll(raw, 255, 1), flags], axis=0)
        h = jnp.maximum(dot(conv_in_ref[:, 0:64], taps.astype(BF16)), 0.0)
        h_ref[z, :, 32:64] = h.astype(BF16).reshape(14, 32, 256)
        h_ref[z, :, 0:32] = pltpu.roll(h, 1, 1).astype(BF16).reshape(14, 32, 256)
        h_ref[z, :, 64:96] = pltpu.roll(h, 255, 1).astype(BF16).reshape(14, 32, 256)
        return carry

    lax.fori_loop(0, 8, first_level, 0)

    def residual(pair, top, count):
        parts = []

        def finish(z):
            total = parts[z][:, 1]
            if z > 0:
                total = total + parts[z - 1][:, 0]
            if z < 7:
                total = total + parts[z + 1][:, 2]
            total = jnp.maximum(total + bias_a, 0.0)
            for n in range(count):
                which = top // 96 + n
                step = (1, 0, 1, 0)[which]
                centre = h_ref[z, 2 * pair + 1 + step, 32:64].astype(F32)
                value = (centre + total[n]).astype(BF16)
                if which in (1, 2):
                    a_ref[z, 2 * pair + step] = value
                else:
                    cut_ref[z, which // 3] = value

        for z in range(8):
            rows = h_ref[z, pl.ds(2 * pair, 4)].reshape(384, 256)
            product = dot(conv_a_ref[top : top + 96 * count], rows)
            parts.append(product.reshape(count, 3, 32, 256))
            if z > 0:
                finish(z - 1)
        finish(7)

    def plain(n, carry):
        residual(n + 2 * lax.div(n, 2), 96, 2)
        return carry

    lax.fori_loop(0, 4, plain, 0)
    residual(2, 0, 3)
    residual(3, 96, 3)

    def pooling(z, carry):
        a = a_ref[z].reshape(6, 2, 32, 256)
        even = jnp.concatenate([a[:, 0].reshape(192, 256), a_ref[z, 4], cut_ref[z, 1]], axis=0)
        late = jnp.concatenate([a[:, 1].reshape(192, 256), cut_ref[z, 0], a_ref[z, 7]], axis=0)
        d = (dot(even, pool_ref[...]) + dot(late, pool_ref[...])).reshape(8, 32, 128)
        pair, half = z // 2, z % 2
        for dx in range(3):
            moved = d if dx == 1 else pltpu.roll(d, 1 if dx == 0 else 127, 2)
            moved = moved.astype(BF16)
            blocks = jnp.concatenate(
                [moved[0:2], moved[6:7], moved[0:6], moved[7:8], moved[4:6]], axis=0
            )
            d_ref[pair, :, 32 * dx : 32 * dx + 32, 128 * half : 128 * half + 128] = blocks
        return carry

    for z in range(8):
        pooling(z, 0)

    def coarse(pair, carry):
        for n, (start, count, late) in enumerate(
            [(3, 3, 0), (4, 3, 0), (5, 3, 0), (6, 3, 0), (0, 3, 0), (1, 2, 0), (9, 2, 1), (9, 3, 0)]
        ):
            rows = d_ref[pair, start : start + count].reshape(96 * count, 256)
            e = dot(conv_d_ref[late, :, 0 : 96 * count], rows)
            e = jnp.maximum(e + bias_d, 0.0).astype(BF16)
            e_ref[pair, n // 4, 48 * (n % 4) : 48 * (n % 4) + 48] = e
        return carry

    lax.fori_loop(0, 4, coarse, 0)

    def head(pair, carry):
        lifted = []
        for kind in range(2):
            q = dot(w_q, e_ref[pair, kind])
            lifted.append(q[0:24] + q[24:48])
        q = jnp.concatenate(lifted, axis=0)
        high = q.astype(BF16).astype(F32)
        low = q - high
        for half in range(2):
            z = 2 * pair + half
            at = slice(128 * half, 128 * half + 128)
            both = jnp.concatenate([high[:, at], low[:, at]], axis=1).astype(BF16)
            up = dot(both, spread_ref[...])
            own = a_ref[z, 2:10].reshape(256, 256)
            other = jnp.concatenate(
                [
                    a_ref[z, 2:5].reshape(96, 256),
                    cut_ref[z].reshape(64, 256),
                    a_ref[z, 7:10].reshape(96, 256),
                ],
                axis=0,
            )
            own = jax.nn.sigmoid(dot(w_o_diag, own) + up[0:24] + bias_o)
            other = jax.nn.sigmoid(dot(w_o_diag, other) + up[24:48] + bias_o)
            for o in range(3):
                s, t = own[8 * o : 8 * o + 8], other[8 * o : 8 * o + 8]
                core = s[:, 0:128] + t[:, 0:128] * weight_y
                beyond = s[:, 128:256] * weight_x + t[:, 128:256] * weight_xy
                out_ref[o, z] = fold(core, beyond) * scale
        return carry

    lax.fori_loop(0, 4, head, 0)


def network(place, order, margins, b_o, got, w_in, b_in, w_a, b_a, w_d, b_d, w_u, w_o, **options):
    smem = pl.BlockSpec(memory_space=pltpu.SMEM)
    vmem = pl.BlockSpec(memory_space=pltpu.VMEM)
    return pl.pallas_call(
        functools.partial(network_kernel, place),
        out_shape=jax.ShapeDtypeStruct((3, 8, 8, 128), F32),
        in_specs=[smem] * 3 + [vmem] * 9,
        out_specs=vmem,
        scratch_shapes=[
            pltpu.VMEM((27, 48, 128), BF16),
            pltpu.VMEM((448, 128), BF16),
            pltpu.VMEM((384, 384), BF16),
            pltpu.VMEM((2, 48, 384), BF16),
            pltpu.VMEM((256, 128), BF16),
            pltpu.VMEM((256, 256), BF16),
            pltpu.VMEM((8, 14, 96, 256), BF16),
            pltpu.VMEM((8, 12, 32, 256), BF16),
            pltpu.VMEM((8, 2, 32, 256), BF16),
            pltpu.VMEM((4, 12, 96, 256), BF16),
            pltpu.VMEM((4, 2, 192, 256), BF16),
        ],
        compiler_params=pltpu.CompilerParams(vmem_limit_bytes=48 * 1024 * 1024),
        **options,
    )(order, margins, b_o, got, w_in, b_in[None], w_a, b_a[None], w_d, b_d[None], w_u, w_o)


def whereabouts():
    return lax.axis_index("gx"), lax.axis_index("gy")


def per_device(raw, section_order, margins, w_in, b_in, w_a, b_a, w_d, b_d, w_u, w_o, b_o):
    got = exchange(raw)
    return network(
        whereabouts, section_order, margins, b_o, got, w_in, b_in, w_a, b_a, w_d, b_d, w_u, w_o
    )


def solution(mesh):
    placed = (P("gy", None, "gx"), P(), P(), P(), P(), P(), P(), P(), P(), P(), P(), P())
    return jax.shard_map(
        per_device, mesh=mesh, in_specs=placed, out_specs=P(None, None, "gx", "gy"), check_vma=False
    )
```

profile of v0, /device:TPU:1, one launch (start us, length us, event | category | flops | bytes accessed | tf_op | source)
XLA Modules:
  0.0 35.5 jit_solution(6567268313348522148)
XLA Ops:
  0.0 0.0 copy-start.9
  0.0 0.0 copy-start.1
  0.0 0.8 %copy.14.margins_ref = s32[16,8]{1,0:T(8,128)S(1)} copy(s32[16,8]{0,1:T(8,128)} %param.14) | data formatting | bytes 1024 | tf_op args[2]
  0.8 0.8 %copy.15.w_in_ref = bf16[28,9]{1,0:T(8,128)(2,1)S(1)} copy(bf16[28,9]{0,1:T(8,128)(2,1)} %param.15) | data formatting | bytes 1008 | tf_op args[3]
  1.6 1.4 %copy.13.raw_ref = bf16[1,128,64]{2,1,0:T(8,128)(2,1)} copy(bf16[1,128,64]{1,2,0:T(8,128)(2,1)} %param.12) | data formatting | bytes 32768 | tf_op args[0]
  3.0 0.0 copy-done.9
  3.0 0.2 copy.16.w_d_ref
  3.2 0.0 copy-start.2
  3.2 0.0 copy-start.3
  3.2 0.0 copy-start.4
  3.2 0.0 copy-start.5
  3.2 0.0 copy-start.6
  3.3 0.0 copy-start.7
  3.3 0.0 copy-start.8
  3.3 18.8 %shard_map.118.got_ref = bf16[4,8,16,128]{3,2,1,0:T(8,128)(2,1)} custom-call(bf16[1,128,64]{2,1,0:T(8,128)(2,1)} %copy.13.raw_ref), custom_call_target="tpu_custom_call" | custom-call | tf_op jit(solution)/shard_map/pallas_call | solution.py:122
  22.1 0.0 copy-done.1
  22.1 0.0 copy-done.2
  22.1 0.0 copy-done.3
  22.1 0.0 copy-done.4
  22.1 0.0 copy-done.5
  22.1 0.0 copy-done.6
  22.1 0.0 copy-done.7
  22.1 0.0 copy-done.8
  22.1 0.0 copy-start
  22.2 0.9 %copy-done = bf16[4,8,16,128]{3,2,1,0:T(8,128)(2,1)S(1)} copy-done((bf16[4,8,16,128]{3,2,1,0:T(8,128)(2,1)S(1)}, bf16[4,8,16,128]{3,2,1,0:T(8,128)(2,1)}, u32[]{:S(2)}) %copy-start) | copy-done | bytes 131096
  23.1 12.5 %shard_map.119 = f32[3,8,8,128]{3,2,1,0:T(8,128)} custom-call(s32[8]{0:T(128)S(1)} %copy-done.4, s32[16,8]{1,0:T(8,128)S(1)} %copy.14.margins_ref, f32[3]{0:T(128)S(1)} %copy-done.5, bf16[4,8,16,128]{3,2,1,0:T(8,128)(2,1)S(1)} %copy-done, bf16[28,9]{1,0:T(8,128)(2,1)S(1)} %copy.15.w_in_ref, f32[1,28]{1,0:T(1,128)S(1)} %bitcast.3, ...), custom_call_target="tpu_custom_call" | custom-call | tf_op jit(solution)/shard_map/pallas_call | solution.py:446
Async XLA Ops:
  0.0 3.0 %copy-start.9 = (bf16[9,36,28]{1,2,0:T(8,128)(2,1)S(1)}, bf16[9,36,28]{1,2,0:T(8,128)(2,1)}, u32[]{:S(2)}) copy-start(bf16[9,36,28]{1,2,0:T(8,128)(2,1)} %param.19) | copy-start | bytes 54436
  0.0 22.1 %copy-start.1 = (bf16[27,28,28]{2,1,0:T(8,128)(2,1)S(1)}, bf16[27,28,28]{2,1,0:T(8,128)(2,1)}, u32[]{:S(2)}) copy-start(bf16[27,28,28]{2,1,0:T(8,128)(2,1)} %w_a_ref.1) | copy-start | bytes 127012
  3.2 18.9 %copy-start.2 = (bf16[28,36]{1,0:T(8,128)(2,1)S(1)}, bf16[28,36]{1,0:T(8,128)(2,1)}, u32[]{:S(2)}) copy-start(bf16[28,36]{1,0:T(8,128)(2,1)} %w_u_ref.1) | copy-start | bytes 6052
  3.2 18.9 %copy-start.3 = (bf16[3,28]{1,0:T(4,128)(2,1)S(1)}, bf16[3,28]{1,0:T(4,128)(2,1)}, u32[]{:S(2)}) copy-start(bf16[3,28]{1,0:T(4,128)(2,1)} %w_o_ref.1) | copy-start | bytes 508
  3.2 18.9 %copy-start.4 = (s32[8]{0:T(128)S(1)}, s32[8]{0:T(128)}, u32[]{:S(2)}) copy-start(s32[8]{0:T(128)} %order_ref.1) | copy-start | bytes 100
  3.2 18.9 %copy-start.5 = (f32[3]{0:T(128)S(1)}, f32[3]{0:T(128)}, u32[]{:S(2)}) copy-start(f32[3]{0:T(128)} %b_o_ref.1) | copy-start | bytes 40
  3.2 18.9 %copy-start.6 = (f32[28]{0:T(128)S(1)}, f32[28]{0:T(128)}, u32[]{:S(2)}) copy-start(f32[28]{0:T(128)} %param.16) | copy-start | bytes 340
  3.3 18.9 %copy-start.7 = (f32[28]{0:T(128)S(1)}, f32[28]{0:T(128)}, u32[]{:S(2)}) copy-start(f32[28]{0:T(128)} %param.18) | copy-start | bytes 340
  3.3 18.9 %copy-start.8 = (f32[36]{0:T(128)S(1)}, f32[36]{0:T(128)}, u32[]{:S(2)}) copy-start(f32[36]{0:T(128)} %param.20) | copy-start | bytes 436
  22.1 0.9 %copy-start = (bf16[4,8,16,128]{3,2,1,0:T(8,128)(2,1)S(1)}, bf16[4,8,16,128]{3,2,1,0:T(8,128)(2,1)}, u32[]{:S(2)}) copy-start(bf16[4,8,16,128]{3,2,1,0:T(8,128)(2,1)} %shard_map.118.got_ref) | copy-start | bytes 393220
where the time goes:
time: 35.8 us; the launch traced here: 35.5 us
  Pallas kernels  31.3 us (87%)
  local copies, waits for them, and re-layouts  4.14 us (12%)
    pallas_call x1, Pallas kernels, exchange(): pl.pallas_call(exchange_kernel, out_shape=jax.ShapeDtypeStruct((4, 8, 16,...  18.8 us
    pallas_call x1, Pallas kernels, network(): pl.pallas_call(functools.partial(network_kernel, place), out_shape=jax.Sh...  12.5 us
    unnamed x24, local copies, waits for them, and re-layouts  4.14 us

commit v1 on v0

v1 whole, which is shorter than its diff:
```python
import functools

import jax
import jax.numpy as jnp
import ml_dtypes
import numpy as np
from jax import lax
from jax.experimental import pallas as pl
from jax.experimental.pallas import tpu as pltpu
from jax.sharding import PartitionSpec as P

MESH = pl.DeviceIdType.MESH
F32 = jnp.float32
BF16 = jnp.bfloat16
BIG = -1e30


def iota(shape, dim):
    return lax.broadcasted_iota(jnp.int32, shape, dim)


def within(x, low, high):
    return (x >= low) & (x <= high)


def dot(a, b):
    return jnp.dot(a, b, preferred_element_type=F32)


def neighbours(gi):
    odd = lax.rem(gi, 2)
    column = lax.div(gi, 2)
    beside = lax.rem(column + 7 + 2 * odd, 8)
    return odd, column, beside


def exchange_kernel(raw_ref, got_ref, send_ref, send_sem, recv_sem):
    gi = lax.axis_index("gx")
    gj = lax.axis_index("gy")
    odd, column, beside = neighbours(gi)
    barrier = pltpu.get_barrier_semaphore()

    def greet(n, carry):
        strip = lax.rem(2 * gj + 15 + lax.rem(n, 4), 16)
        slab = lax.div(n, 4)

        @pl.when((strip != gi) | (slab != gj))
        def _():
            pl.semaphore_signal(barrier, inc=1, device_id=(strip, slab), device_id_type=MESH)

        return carry

    lax.fori_loop(0, 32, greet, 0)

    row = iota((256, 128), 0)
    rows = (iota((256, 128), 1) == 8 * (row // 16) - 4 + row % 16).astype(F32).astype(BF16)
    lane = iota((64, 256), 1)
    tile = lane % 128
    even_main = jnp.where(tile < 64, tile, jnp.where(tile >= 122, tile - 122, -1))
    odd_main = jnp.where(tile >= 64, tile - 64, jnp.where(tile < 6, tile + 58, -1))
    even_side = jnp.where(within(tile, 6, 9), tile - 6, -1)
    odd_side = jnp.where(within(tile, 118, 121), tile - 58, -1)
    ends = (gi == 0) | (gi == 15)
    main = jnp.where(odd == 1, odd_main, even_main)
    side = jnp.where(ends, -1, jnp.where(odd == 1, odd_side, even_side))
    cols = (iota((64, 256), 0) == jnp.where(lane < 128, main, side)).astype(F32).astype(BF16)
    picked = lax.dot_general(
        rows, raw_ref[0], (((1,), (1,)), ((), ())), preferred_element_type=F32
    ).astype(BF16)
    message = dot(picked, cols).astype(BF16)
    send_ref[0:16] = message[:, 0:128].reshape(16, 16, 128)
    send_ref[16:32] = message[:, 128:256].reshape(16, 16, 128)

    at_home = (gj == column) | (gj == beside)

    @pl.when(at_home)
    def _():
        pl.semaphore_wait(barrier, 31)

    @pl.when(jnp.logical_not(at_home))
    def _():
        pl.semaphore_wait(barrier, 32)

    def send(n, carry):
        target = lax.rem(gi + n, 16)
        for kind in range(2):
            where_to = column if kind == 0 else beside
            slot = odd if kind == 0 else 3 - odd
            source = send_ref.at[target + 16 * kind]
            place = got_ref.at[slot, gj]
            here = (target == gi) & (where_to == gj)

            @pl.when(here)
            def _():
                pltpu.make_async_copy(source, place, recv_sem).start()

            @pl.when(jnp.logical_not(here))
            def _():
                pltpu.make_async_remote_copy(
                    src_ref=source,
                    dst_ref=place,
                    send_sem=send_sem,
                    recv_sem=recv_sem,
                    device_id=(target, where_to),
                    device_id_type=MESH,
                ).start()

        return carry

    lax.fori_loop(0, 16, send, 0)
    pltpu.make_async_copy(got_ref, got_ref, recv_sem).wait()

    @pl.when(at_home)
    def _():
        pltpu.make_async_copy(send_ref.at[0:31], send_ref.at[0:31], send_sem).wait()

    @pl.when(jnp.logical_not(at_home))
    def _():
        pltpu.make_async_copy(send_ref, send_ref, send_sem).wait()


def exchange(raw):
    return pl.pallas_call(
        exchange_kernel,
        out_shape=jax.ShapeDtypeStruct((4, 8, 16, 128), BF16),
        in_specs=[pl.BlockSpec(memory_space=pltpu.VMEM)],
        out_specs=pl.BlockSpec(memory_space=pl.ANY),
        scratch_shapes=[
            pltpu.VMEM((32, 16, 128), BF16),
            pltpu.SemaphoreType.DMA,
            pltpu.SemaphoreType.DMA,
        ],
        compiler_params=pltpu.CompilerParams(collective_id=0, has_side_effects=True),
    )(jnp.transpose(raw, (0, 2, 1)))


def tiled_taps(pad_ref, first, taps):
    tiles = []
    for start in range(0, taps, 4):
        tile = None
        for q in range(min(4, taps - start)):
            part = pad_ref[first + start + q].astype(F32)
            part = part if q == 0 else pltpu.roll(part, 32 * q, 1)
            tile = part if tile is None else tile + part
        tiles.append(tile)
    return jnp.concatenate(tiles, axis=1)


def as_column(row, size):
    shape = (size, row.shape[1])
    return jnp.sum(jnp.where(iota(shape, 0) == iota(shape, 1), row, 0.0), axis=1, keepdims=True)


def split(x):
    high = x.astype(BF16)
    return high, (x - high.astype(F32)).astype(BF16)


def pooling_table():
    core = np.zeros((2, 128, 3, 128), np.float32)
    side = np.zeros((128, 5, 3, 128), np.float32)

    def add(pair, dx, lane, section, coarse, left, right):
        for fine in (2 * coarse, 2 * coarse + 1):
            if left and -2 <= fine <= 3:
                side[16 * section + fine + 2, pair, dx, lane] = 0.25
            elif right and 124 <= fine <= 129:
                side[16 * section + 10 + fine - 124, pair, dx, lane] = 0.25
            elif not left and not right:
                core[section % 2, fine, dx, lane] = 0.25

    for section in range(8):
        for dx in range(3):
            for m in range(64):
                at = m + dx - 1
                add(section // 2, dx, 64 * (section % 2) + m, section, at, at < 0, at > 63)
            for n, m in enumerate((0, 1, 62, 63)):
                add(4, dx, 4 * section + n, section, m + dx - 1, n < 2, n >= 2)
    core = np.concatenate([np.concatenate([core[n], core[n]]) for n in range(2)]).reshape(512, 384)
    side = np.concatenate([side, side]).reshape(256, 5 * 384)
    return core.astype(ml_dtypes.bfloat16), side.astype(ml_dtypes.bfloat16)


def network_kernel(
    place,
    order_ref,
    margins_ref,
    b_o_ref,
    got_ref,
    w_in_ref,
    b_in_ref,
    w_a_ref,
    b_a_ref,
    w_d_ref,
    b_d_ref,
    w_u_ref,
    w_o_ref,
    pool_core_ref,
    pool_side_ref,
    out_ref,
    pad_ref,
    conv_in_ref,
    conv_a_ref,
    conv_d_ref,
    raw_ref,
    h_ref,
    a_ref,
    d_ref,
    e_ref,
):
    gi, gj = place()

    pad_ref[...] = jnp.zeros_like(pad_ref)
    pad_ref[0:27, 0:28, 0:28] = w_a_ref[...]
    lane = iota((32, 512), 1)
    for dz in range(3):
        taps = tiled_taps(pad_ref, 9 * dz, 9)
        taps = jnp.concatenate([taps, jnp.zeros((32, 128), F32)], axis=1)
        for n in range(5):
            moved = taps if n in (1, 4) else pltpu.roll(taps, 96 if n == 2 else 192, 1)
            if n == 0:
                moved = jnp.where(lane < 384, moved, 0.0)
            if n == 4:
                moved = jnp.where(lane >= 96, moved, 0.0)
            conv_a_ref[96 * n + 32 * dz : 96 * n + 32 * dz + 32] = moved.astype(BF16)
    pad_ref[0:9] = jnp.zeros((9, 32, 128), BF16)
    pad_ref[0:9, 0:28, 0:36] = w_d_ref[...]
    taps = pad_ref[0:12].astype(F32).reshape(384, 128)
    taps = jnp.where(iota((384, 128), 0) < 288, taps, 0.0)
    taps = jnp.concatenate([taps[128 * n : 128 * n + 128].T[0:40] for n in range(3)], axis=1)
    taps = jnp.concatenate([taps, jnp.zeros((40, 384), F32)], axis=1)
    lane = iota((40, 768), 1)
    for n in range(8):
        if n < 4:
            moved = taps if n == 0 else pltpu.roll(taps, 96 * n, 1)
        elif n == 4:
            moved = jnp.where(lane < 192, taps, 0.0) + jnp.where(
                lane >= 576, pltpu.roll(taps, 384, 1), 0.0
            )
        elif n == 5:
            moved = jnp.where(within(lane, 96, 191), pltpu.roll(taps, 96, 1), 0.0) + jnp.where(
                within(lane, 576, 671), pltpu.roll(taps, 480, 1), 0.0
            )
        elif n == 6:
            moved = jnp.where(within(lane, 384, 479), pltpu.roll(taps, 192, 1), 0.0) + jnp.where(
                lane >= 672, pltpu.roll(taps, 576, 1), 0.0
            )
        else:
            moved = jnp.where(within(lane, 384, 575), pltpu.roll(taps, 288, 1), 0.0) + jnp.where(
                lane >= 672, pltpu.roll(taps, 672, 1), 0.0
            )
        conv_d_ref[40 * n : 40 * n + 40] = moved
    bias_a = as_column(b_a_ref[...], 32)
    bias_d = jnp.concatenate([as_column(b_d_ref[...], 40)] * 8, axis=0)

    pad_ref[0] = jnp.zeros((32, 128), BF16)
    pad_ref[0, 0:9, 0:28] = w_in_ref[...]
    tap = iota((32, 128), 0)
    lane = iota((32, 128), 1)
    put = (lane == 16 * (tap % 3) + tap // 3) & (tap < 9)
    base = lax.dot_general(
        pad_ref[0],
        put.astype(F32).astype(BF16),
        (((0,), (0,)), ((), ())),
        preferred_element_type=F32,
    )[0:32]
    bias = as_column(b_in_ref[...], 32)
    rest = bias
    extra = jnp.where(lane == 51, BIG, 0.0)
    for n in range(3):
        part = rest.astype(BF16).astype(F32)
        extra = extra + jnp.where(lane == 48 + n, part, 0.0)
        rest = rest - part
    for y in range(14):
        taps = extra + (base if y == 0 else pltpu.roll(base, y, 1))
        if y < 3:
            taps = taps + jnp.where(lane == 52, BIG, 0.0)
        if y >= 11:
            taps = taps + jnp.where(lane == 53, BIG, 0.0)
        conv_in_ref[32 * y : 32 * y + 32] = taps.astype(BF16)

    w_o = w_o_ref[...].astype(F32)
    w_o = jnp.concatenate([jnp.broadcast_to(w_o[o : o + 1], (8, 28)) for o in range(3)], axis=0)
    w_o = jnp.concatenate([w_o, jnp.zeros((24, 4), F32)], axis=1)
    pad_ref[0] = jnp.zeros((32, 128), BF16)
    pad_ref[0, 0:28, 0:36] = w_u_ref[...]
    w_u = pad_ref[0].astype(F32)
    w_u = jnp.concatenate([w_u, jnp.zeros_like(w_u)], axis=1)
    w_u = w_u + pltpu.roll(w_u, 40, 1)
    w_u = w_u + pltpu.roll(w_u, 80, 1)
    w_q = dot(w_o.astype(BF16), w_u.astype(BF16))
    lane = iota((24, 256), 1)
    w_q = jnp.where(lane // 40 == (iota((24, 256), 0) % 8) // 2, w_q, 0.0)[:, 0:160]
    w_q_high, w_q_low = split(w_q)
    w_q = jnp.concatenate([w_q_high.astype(F32), w_q_low.astype(F32)], axis=0).astype(BF16)
    w_o = jnp.concatenate([w_o] * 12, axis=1)
    w_o = jnp.concatenate([w_o, w_o], axis=0)
    lane = iota((48, 384), 1) // 32
    row = iota((48, 384), 0)
    block = jnp.where(row < 24, row % 8, jnp.where(within(row % 8, 3, 4), row % 8 + 5, row % 8))
    w_o = jnp.where(lane == block, w_o, 0.0).astype(BF16)[:, 0:320]
    row = iota((48, 1), 0) % 24
    bias_o = jnp.where(row < 8, b_o_ref[0], jnp.where(row < 16, b_o_ref[1], b_o_ref[2]))

    row = iota((256, 256), 0) % 128
    spread = (row == iota((256, 256), 1) // 2).astype(F32).astype(BF16)
    row = iota((256, 128), 0) % 128
    lane = iota((256, 128), 1)
    which = jnp.where(
        within(lane % 16, 2, 5), lane % 16 // 2 - 1, jnp.where(within(lane % 16, 10, 13), lane % 16 // 2 - 3, -999)
    )
    spread_side = (row == 4 * (lane // 16) + which).astype(F32).astype(BF16)

    def margin(step_y, step_x):
        y, x = gi + step_y, gj + step_x
        inside = (y >= 0) & (y < 16) & (x >= 0) & (x < 8)
        value = margins_ref[jnp.clip(x, 0, 7), jnp.clip(y, 0, 15)]
        return value.astype(F32), jnp.where(inside, 1.0, 0.0)

    def ramp(distance, width):
        return jnp.clip(1.0 - distance / (width + 1.0), 0.0, 1.0)

    y = iota((8, 128), 0)
    lane = iota((8, 128), 1)
    upper = y < 4
    off_y = jnp.where(upper, y + 1, 8 - y).astype(F32)
    nth = lane % 16
    leftward = nth < 8
    off_x = jnp.where(
        within(nth, 2, 5), nth - 1, jnp.where(within(nth, 10, 13), 14 - nth, 99)
    ).astype(F32)

    def by_place(pairs):
        m = jnp.where(leftward, pairs[0][0], pairs[1][0])
        there = jnp.where(leftward, pairs[0][1], pairs[1][1])
        return m, there

    m_up, in_up = margin(-1, 0)
    m_down, in_down = margin(1, 0)
    weight_y = ramp(off_y, jnp.where(upper, m_up, m_down)) * jnp.where(upper, in_up, in_down)
    m, there = by_place((margin(0, -1), margin(0, 1)))
    weight_x = ramp(off_x, m) * there
    m_top, there_top = by_place((margin(-1, -1), margin(-1, 1)))
    m_low, there_low = by_place((margin(1, -1), margin(1, 1)))
    m = jnp.where(upper, m_top, m_low)
    weight_xy = ramp(off_y, m) * ramp(off_x, m) * jnp.where(upper, there_top, there_low)

    def fold(core, beyond, z):
        left = jnp.where(lane < 4, pltpu.roll(beyond, (126 - 16 * z) % 128, 1), 0.0)
        right = jnp.where(lane >= 124, pltpu.roll(beyond, (114 - 16 * z) % 128, 1), 0.0)
        return core + left + right

    scale = 1.0 / fold(1.0 + weight_y, weight_x + weight_xy, 0)

    tile = iota((16, 128), 1)
    sides = [jnp.zeros((16, 128), F32) for _ in range(5)]
    for z in range(8):
        slab = jnp.int32(0)
        for k in range(8):
            slab = slab + jnp.where(order_ref[k] == z, k, 0)
        near, far, before, after = [got_ref[n, slab].astype(F32) for n in range(4)]
        core = jnp.where(tile < 64, near, far)
        low = jnp.where(tile < 6, far, after)
        high = jnp.where(tile >= 122, near, before)
        beside = jnp.where(tile < 64, low, high)
        for n in range(5):
            s = n - 2
            moved = core if s == 0 else pltpu.roll(core, -s % 128, 1)
            if s > 0:
                moved = jnp.where(tile >= 128 - s, pltpu.roll(beside, 122 - s, 1), moved)
            if s < 0:
                moved = jnp.where(tile < -s, pltpu.roll(beside, 6 - s, 1), moved)
            raw_ref[16 * n : 16 * n + 16, 128 * z : 128 * z + 128] = moved.astype(BF16)
            moved = pltpu.roll(beside, (16 * z + 8 - s) % 128, 1)
            sides[n] = jnp.where(tile // 16 == z, moved, sides[n])
    for n in range(5):
        raw_ref[16 * n : 16 * n + 16, 1024:1152] = sides[n].astype(BF16)

    def flags(dx, side):
        kind = iota((16, 128), 0)
        nth = tile % 16
        if side:
            column = jnp.where(nth < 8, nth - 3 + dx, 113 + nth + dx)
            cut = jnp.where(nth < 8, 4, 123)
            outside = column == cut
        else:
            column = tile + dx - 1
            outside = tile < 0
        outside = outside | ((column < 0) & (gj == 0)) | ((column > 127) & (gj == 7))
        value = jnp.where(kind < 3, 1.0, 0.0)
        value = jnp.where((kind == 3) & outside, 1.0, value)
        value = jnp.where((kind == 4) & (gi == 0), 1.0, value)
        return jnp.where((kind == 5) & (gi == 15), 1.0, value).astype(BF16)

    for dx in range(3):
        flag = flags(dx, False)
        flag = jnp.concatenate([flag, flag], axis=1)
        for q in range(5):
            at = slice(256 * q, 256 * q + 256) if q < 4 else slice(1024, 1152)
            taps = jnp.concatenate(
                [raw_ref[16 * dx : 16 * dx + 48, at], flag if q < 4 else flags(dx, True)], axis=0
            )
            h = jnp.maximum(dot(conv_in_ref[:, 0:64], taps).astype(BF16), 0)
            h_ref[:, dx, :, at] = h.reshape(14, 32, h.shape[1])

    def residual(three):
        extra = three in (1, 2)
        first = 0 if three == 1 else 1
        names = [None, 3 * three, 3 * three + 1, 3 * three + 2, None]
        names[0], names[4] = 10, 11
        names = [n if n < 10 or k in (0, 4) else n + 2 for k, n in enumerate(names)]
        count = 4 if extra else 3
        lane = iota((count, 32, 128), 2)

        def finish(total, at):
            total = jnp.maximum(total + bias_a, 0.0)
            for n in range(count):
                which = first + n
                step = (2, 0, 1, 2, 0)[which]
                centre = h_ref[3 * three + 1 + step, 1, :, at].astype(F32)
                a_ref[names[which], :, at] = (centre + total[n]).astype(BF16)

        parts = []
        for q in range(5):
            at = slice(256 * q, 256 * q + 256) if q < 4 else slice(1024, 1152)
            rows = h_ref[3 * three : 3 * three + 5, :, :, at].reshape(480, at.stop - at.start)
            product = dot(conv_a_ref[96 * first : 96 * (first + count), 0:480], rows)
            product = product.reshape(count, 3, 32, at.stop - at.start)
            if q == 4:
                total = product[:, 1]
                total = total + jnp.where(lane >= 16, pltpu.roll(product[:, 0], 16, 2), 0.0)
                total = total + jnp.where(lane < 112, pltpu.roll(product[:, 2], 112, 2), 0.0)
                finish(total, at)
                break
            for half in range(2):
                parts.append(product[:, :, :, 128 * half : 128 * half + 128])
                z = len(parts) - 2
                if z >= 0:
                    total = parts[z][:, 1] + parts[z + 1][:, 2]
                    if z > 0:
                        total = total + parts[z - 1][:, 0]
                    finish(total, slice(128 * z, 128 * z + 128))
        finish(parts[7][:, 1] + parts[6][:, 0], slice(896, 1024))

    for three in range(4):
        residual(three)

    def pooled_rows(at):
        even = jnp.concatenate([a_ref[n, :, at] for n in (0, 2, 4, 6, 8, 12, 4, 11)], axis=0)
        late = jnp.concatenate([a_ref[n, :, at] for n in (1, 3, 5, 7, 9, 13, 10, 7)], axis=0)
        return jnp.concatenate([even, late], axis=1)

    side = pooled_rows(slice(1024, 1152))
    for q in range(5):
        d = dot(side, pool_side_ref[:, 384 * q : 384 * q + 384])
        if q < 4:
            for half in range(2):
                z = 2 * q + half
                core = pooled_rows(slice(128 * z, 128 * z + 128))
                d = d + dot(core, pool_core_ref[256 * half : 256 * half + 256])
        for dx in range(3):
            part = d[:, 128 * dx : 128 * dx + 128].astype(BF16)
            d_ref[:, dx, :, 128 * q : 128 * q + 128] = part.reshape(8, 32, 128)

    conv_d = conv_d_ref[...].astype(BF16)
    for at in (slice(0, 256), slice(256, 512), slice(512, 640)):
        e = dot(conv_d, d_ref[:, :, :, at].reshape(768, at.stop - at.start))
        e_ref[:, at] = jnp.maximum(e + bias_d, 0.0).astype(BF16)

    lifted = []
    for kind in range(2):
        q = dot(w_q, e_ref[160 * kind : 160 * kind + 160])
        lifted.append(q[0:24] + q[24:48])
    q = jnp.concatenate(lifted, axis=0)
    high = q.astype(BF16).astype(F32)
    low = q - high

    def both(n):
        at = slice(128 * n, 128 * n + 128)
        return jnp.concatenate([high[:, at], low[:, at]], axis=1).astype(BF16)

    def logits(at):
        return dot(w_o, a_ref[2:12, :, at].reshape(320, at.stop - at.start)) + bias_o

    at = slice(1024, 1152)
    beyond = jax.nn.sigmoid(logits(at) + dot(both(4), spread_side))
    beyond = [
        beyond[8 * o : 8 * o + 8] * weight_x + beyond[24 + 8 * o : 32 + 8 * o] * weight_xy
        for o in range(3)
    ]
    up = dot(jnp.concatenate([both(n) for n in range(4)], axis=0), spread)
    for n in range(4):
        at = slice(256 * n, 256 * n + 256)
        s = jax.nn.sigmoid(logits(at) + up[48 * n : 48 * n + 48])
        for half in range(2):
            z = 2 * n + half
            for o in range(3):
                own = s[8 * o : 8 * o + 8, 128 * half : 128 * half + 128]
                other = s[24 + 8 * o : 32 + 8 * o, 128 * half : 128 * half + 128]
                out_ref[o, z] = fold(own + other * weight_y, beyond[o], z) * scale


def network(place, order, margins, b_o, got, w_in, b_in, w_a, b_a, w_d, b_d, w_u, w_o, **options):
    smem = pl.BlockSpec(memory_space=pltpu.SMEM)
    vmem = pl.BlockSpec(memory_space=pltpu.VMEM)
    return pl.pallas_call(
        functools.partial(network_kernel, place),
        out_shape=jax.ShapeDtypeStruct((3, 8, 8, 128), F32),
        in_specs=[smem] * 3 + [vmem] * 11,
        out_specs=vmem,
        scratch_shapes=[
            pltpu.VMEM((27, 32, 128), BF16),
            pltpu.VMEM((448, 128), BF16),
            pltpu.VMEM((480, 512), BF16),
            pltpu.VMEM((320, 768), F32),
            pltpu.VMEM((80, 1152), BF16),
            pltpu.VMEM((14, 3, 32, 1152), BF16),
            pltpu.VMEM((14, 32, 1152), BF16),
            pltpu.VMEM((8, 3, 32, 640), BF16),
            pltpu.VMEM((320, 640), BF16),
        ],
        compiler_params=pltpu.CompilerParams(vmem_limit_bytes=48 * 1024 * 1024),
        **options,
    )(
        order,
        margins.T,
        b_o,
        got,
        w_in.T,
        b_in[None],
        w_a,
        b_a[None],
        jnp.transpose(w_d, (0, 2, 1)),
        b_d[None],
        w_u,
        w_o,
        *pooling_table(),
    )


def whereabouts():
    return lax.axis_index("gx"), lax.axis_index("gy")


def per_device(raw, section_order, margins, w_in, b_in, w_a, b_a, w_d, b_d, w_u, w_o, b_o):
    got = exchange(raw)
    return network(
        whereabouts, section_order, margins, b_o, got, w_in, b_in, w_a, b_a, w_d, b_d, w_u, w_o
    )


def solution(mesh):
    placed = (P("gy", None, "gx"), P(), P(), P(), P(), P(), P(), P(), P(), P(), P(), P())
    return jax.shard_map(
        per_device, mesh=mesh, in_specs=placed, out_specs=P(None, None, "gx", "gy"), check_vma=False
    )
```

time: 35.8 us -> 29.7 us (0.83)
  Pallas kernels: 31.3 us -> 25.2 us
    pallas_call x1, Pallas kernels: 12.5 us -> 6.45 us  [network(): pl.pallas_call(functools.partial(network_kernel, place), out_shape=jax.Sh...]
    unnamed x24 -> x28, local copies, waits for them, and re-layouts: 4.14 us -> 4.07 us
where the time goes in v1:
time: 29.7 us; the launch traced here: 29.5 us
  Pallas kernels  25.2 us (85%)
  local copies, waits for them, and re-layouts  4.07 us (14%)
    pallas_call x1, Pallas kernels, exchange(): pl.pallas_call(exchange_kernel, out_shape=jax.ShapeDtypeStruct((4, 8, 16,...  18.8 us
    pallas_call x1, Pallas kernels, network(): pl.pallas_call(functools.partial(network_kernel, place), out_shape=jax.Sh...  6.45 us
    unnamed x28, local copies, waits for them, and re-layouts  4.07 us

profile of v1, /device:TPU:1, one launch (start us, length us, event | category | flops | bytes accessed | tf_op | source)
XLA Modules:
  0.0 29.5 jit_solution(11027632442214049065)
XLA Ops:
  0.0 0.0 copy-start.4
  0.0 0.0 copy-start.5
  0.0 0.0 copy-start.6
  0.0 0.0 copy-start.7
  0.0 0.0 copy-start.8
  0.0 0.0 copy-start.9
  0.0 0.0 copy-start.10
  0.0 0.0 copy-start.11
  0.1 0.0 copy-start.12
  0.1 0.0 copy-start.13
  0.1 18.8 %shard_map.136.got_ref = bf16[4,8,16,128]{3,2,1,0:T(8,128)(2,1)} custom-call(bf16[1,64,128]{2,1,0:T(8,128)(2,1)} %bitcast.13), custom_call_target="tpu_custom_call" | custom-call | tf_op jit(solution)/shard_map/pallas_call | solution.py:123
  18.9 0.0 copy-done.4
  18.9 0.0 copy-done.5
  18.9 0.0 copy-done.6
  18.9 0.0 copy-done.7
  18.9 0.0 copy-done.8
  18.9 0.0 copy-done.9
  18.9 0.0 copy-done.10
  18.9 0.0 copy-done.11
  18.9 0.0 copy-done.12
  19.0 0.0 copy-done.13
  19.0 0.0 copy-start
  19.0 1.2 %copy-done = bf16[256,1920]{1,0:T(8,128)(2,1)S(1)} copy-done((bf16[256,1920]{1,0:T(8,128)(2,1)S(1)}, bf16[256,1920]{1,0:T(8,128)(2,1)}, u32[]{:S(2)}) %copy-start) | copy-done | bytes 983064
  20.2 0.0 copy-start.1
  20.2 0.9 %copy-done.1 = bf16[4,8,16,128]{3,2,1,0:T(8,128)(2,1)S(1)} copy-done((bf16[4,8,16,128]{3,2,1,0:T(8,128)(2,1)S(1)}, bf16[4,8,16,128]{3,2,1,0:T(8,128)(2,1)}, u32[]{:S(2)}) %copy-start.1) | copy-done | bytes 131096
  21.1 0.0 copy-start.2
  21.1 1.0 %copy-done.2 = bf16[512,384]{1,0:T(8,128)(2,1)S(1)} copy-done((bf16[512,384]{1,0:T(8,128)(2,1)S(1)}, bf16[512,384]{1,0:T(8,128)(2,1)}, u32[]{:S(2)}) %copy-start.2) | copy-done | bytes 393240
  22.1 0.0 copy-start.3
  22.1 0.9 %copy-done.3 = bf16[27,28,28]{2,1,0:T(8,128)(2,1)S(1)} copy-done((bf16[27,28,28]{2,1,0:T(8,128)(2,1)S(1)}, bf16[27,28,28]{2,1,0:T(8,128)(2,1)}, u32[]{:S(2)}) %copy-start.3) | copy-done | bytes 42360
  23.0 6.5 %shard_map.137 = f32[3,8,8,128]{3,2,1,0:T(8,128)} custom-call(s32[8]{0:T(128)S(1)} %copy-done.9, s32[8,16]{1,0:T(8,128)S(1)} %bitcast.8, f32[3]{0:T(128)S(1)} %copy-done.10, bf16[4,8,16,128]{3,2,1,0:T(8,128)(2,1)S(1)} %copy-done.1, bf16[9,28]{1,0:T(8,128)(2,1)S(1)} %bitcast.9, f32[1,28]{1,0:T(1,128)S(1)} %bitcast.10, bf16[27,28,28]{2,1,0:T(8,128)(2,1)S(1)} %copy-done.3, ...), custom_call_target="tpu_custom_call" | custom-call | tf_op jit(solution)/shard_map/pallas_call | solution.py:506
Async XLA Ops:
  0.0 18.9 %copy-start.4 = (bf16[9,36,28]{1,2,0:T(8,128)(2,1)S(1)}, bf16[9,36,28]{1,2,0:T(8,128)(2,1)}, u32[]{:S(2)}) copy-start(bf16[9,36,28]{1,2,0:T(8,128)(2,1)} %param.21) | copy-start | bytes 54436
  0.0 18.9 %copy-start.5 = (bf16[28,36]{1,0:T(8,128)(2,1)S(1)}, bf16[28,36]{1,0:T(8,128)(2,1)}, u32[]{:S(2)}) copy-start(bf16[28,36]{1,0:T(8,128)(2,1)} %w_u_ref.1) | copy-start | bytes 6052
  0.0 18.9 %copy-start.6 = (s32[16,8]{0,1:T(8,128)S(1)}, s32[16,8]{0,1:T(8,128)}, u32[]{:S(2)}) copy-start(s32[16,8]{0,1:T(8,128)} %param.16) | copy-start | bytes 1540
  0.0 18.9 %copy-start.7 = (bf16[28,9]{0,1:T(8,128)(2,1)S(1)}, bf16[28,9]{0,1:T(8,128)(2,1)}, u32[]{:S(2)}) copy-start(bf16[28,9]{0,1:T(8,128)(2,1)} %param.17) | copy-start | bytes 1516
  0.0 18.9 %copy-start.8 = (bf16[3,28]{1,0:T(4,128)(2,1)S(1)}, bf16[3,28]{1,0:T(4,128)(2,1)}, u32[]{:S(2)}) copy-start(bf16[3,28]{1,0:T(4,128)(2,1)} %w_o_ref.1) | copy-start | bytes 508
  0.0 18.9 %copy-start.9 = (s32[8]{0:T(128)S(1)}, s32[8]{0:T(128)}, u32[]{:S(2)}) copy-start(s32[8]{0:T(128)} %order_ref.1) | copy-start | bytes 100
  0.0 18.9 %copy-start.10 = (f32[3]{0:T(128)S(1)}, f32[3]{0:T(128)}, u32[]{:S(2)}) copy-start(f32[3]{0:T(128)} %b_o_ref.1) | copy-start | bytes 40
  0.0 18.9 %copy-start.11 = (f32[28]{0:T(128)S(1)}, f32[28]{0:T(128)}, u32[]{:S(2)}) copy-start(f32[28]{0:T(128)} %param.18) | copy-start | bytes 340
  0.1 18.9 %copy-start.12 = (f32[28]{0:T(128)S(1)}, f32[28]{0:T(128)}, u32[]{:S(2)}) copy-start(f32[28]{0:T(128)} %param.20) | copy-start | bytes 340
  0.1 18.9 %copy-start.13 = (f32[36]{0:T(128)S(1)}, f32[36]{0:T(128)}, u32[]{:S(2)}) copy-start(f32[36]{0:T(128)} %param.22) | copy-start | bytes 436
  19.0 1.2 %copy-start = (bf16[256,1920]{1,0:T(8,128)(2,1)S(1)}, bf16[256,1920]{1,0:T(8,128)(2,1)}, u32[]{:S(2)}) copy-start(bf16[256,1920]{1,0:T(8,128)(2,1)} %constant.5.clone.pool_side_ref) | copy-start | bytes 2949124
  20.2 0.9 %copy-start.1 = (bf16[4,8,16,128]{3,2,1,0:T(8,128)(2,1)S(1)}, bf16[4,8,16,128]{3,2,1,0:T(8,128)(2,1)}, u32[]{:S(2)}) copy-start(bf16[4,8,16,128]{3,2,1,0:T(8,128)(2,1)} %shard_map.136.got_ref) | copy-start | bytes 393220
  21.1 1.0 %copy-start.2 = (bf16[512,384]{1,0:T(8,128)(2,1)S(1)}, bf16[512,384]{1,0:T(8,128)(2,1)}, u32[]{:S(2)}) copy-start(bf16[512,384]{1,0:T(8,128)(2,1)} %constant.4.clone.pool_core_ref) | copy-start | bytes 1179652
  22.1 0.9 %copy-start.3 = (bf16[27,28,28]{2,1,0:T(8,128)(2,1)S(1)}, bf16[27,28,28]{2,1,0:T(8,128)(2,1)}, u32[]{:S(2)}) copy-start(bf16[27,28,28]{2,1,0:T(8,128)(2,1)} %w_a_ref.1) | copy-start | bytes 127012

commit v2 on v1

--- a/solution.py
+++ b/solution.py
@@ -34,104 +34,9 @@
     return odd, column, beside
 
 
-def exchange_kernel(raw_ref, got_ref, send_ref, send_sem, recv_sem):
-    gi = lax.axis_index("gx")
-    gj = lax.axis_index("gy")
-    odd, column, beside = neighbours(gi)
-    barrier = pltpu.get_barrier_semaphore()
-
-    def greet(n, carry):
-        strip = lax.rem(2 * gj + 15 + lax.rem(n, 4), 16)
-        slab = lax.div(n, 4)
-
-        @pl.when((strip != gi) | (slab != gj))
-        def _():
-            pl.semaphore_signal(barrier, inc=1, device_id=(strip, slab), device_id_type=MESH)
-
-        return carry
-
-    lax.fori_loop(0, 32, greet, 0)
-
-    row = iota((256, 128), 0)
-    rows = (iota((256, 128), 1) == 8 * (row // 16) - 4 + row % 16).astype(F32).astype(BF16)
-    lane = iota((64, 256), 1)
-    tile = lane % 128
-    even_main = jnp.where(tile < 64, tile, jnp.where(tile >= 122, tile - 122, -1))
-    odd_main = jnp.where(tile >= 64, tile - 64, jnp.where(tile < 6, tile + 58, -1))
-    even_side = jnp.where(within(tile, 6, 9), tile - 6, -1)
-    odd_side = jnp.where(within(tile, 118, 121), tile - 58, -1)
-    ends = (gi == 0) | (gi == 15)
-    main = jnp.where(odd == 1, odd_main, even_main)
-    side = jnp.where(ends, -1, jnp.where(odd == 1, odd_side, even_side))
-    cols = (iota((64, 256), 0) == jnp.where(lane < 128, main, side)).astype(F32).astype(BF16)
-    picked = lax.dot_general(
-        rows, raw_ref[0], (((1,), (1,)), ((), ())), preferred_element_type=F32
-    ).astype(BF16)
-    message = dot(picked, cols).astype(BF16)
-    send_ref[0:16] = message[:, 0:128].reshape(16, 16, 128)
-    send_ref[16:32] = message[:, 128:256].reshape(16, 16, 128)
-
-    at_home = (gj == column) | (gj == beside)
-
-    @pl.when(at_home)
-    def _():
-        pl.semaphore_wait(barrier, 31)
-
-    @pl.when(jnp.logical_not(at_home))
-    def _():
-        pl.semaphore_wait(barrier, 32)
-
-    def send(n, carry):
-        target = lax.rem(gi + n, 16)
-        for kind in range(2):
-            where_to = column if kind == 0 else beside
-            slot = odd if kind == 0 else 3 - odd
-            source = send_ref.at[target + 16 * kind]
-            place = got_ref.at[slot, gj]
-            here = (target == gi) & (where_to == gj)
-
-            @pl.when(here)
-            def _():
-                pltpu.make_async_copy(source, place, recv_sem).start()
-
-            @pl.when(jnp.logical_not(here))
-            def _():
-                pltpu.make_async_remote_copy(
-                    src_ref=source,
-                    dst_ref=place,
-                    send_sem=send_sem,
-                    recv_sem=recv_sem,
-                    device_id=(target, where_to),
-                    device_id_type=MESH,
-                ).start()
-
-        return carry
-
-    lax.fori_loop(0, 16, send, 0)
-    pltpu.make_async_copy(got_ref, got_ref, recv_sem).wait()
-
-    @pl.when(at_home)
-    def _():
-        pltpu.make_async_copy(send_ref.at[0:31], send_ref.at[0:31], send_sem).wait()
-
-    @pl.when(jnp.logical_not(at_home))
-    def _():
-        pltpu.make_async_copy(send_ref, send_ref, send_sem).wait()
-
-
-def exchange(raw):
-    return pl.pallas_call(
-        exchange_kernel,
-        out_shape=jax.ShapeDtypeStruct((4, 8, 16, 128), BF16),
-        in_specs=[pl.BlockSpec(memory_space=pltpu.VMEM)],
-        out_specs=pl.BlockSpec(memory_space=pl.ANY),
-        scratch_shapes=[
-            pltpu.VMEM((32, 16, 128), BF16),
-            pltpu.SemaphoreType.DMA,
-            pltpu.SemaphoreType.DMA,
-        ],
-        compiler_params=pltpu.CompilerParams(collective_id=0, has_side_effects=True),
-    )(jnp.transpose(raw, (0, 2, 1)))
+def as_column(row, size):
+    shape = (size, row.shape[1])
+    return jnp.sum(jnp.where(iota(shape, 0) == iota(shape, 1), row, 0.0), axis=1, keepdims=True)
 
 
 def tiled_taps(pad_ref, first, taps):
@@ -146,47 +51,8 @@
     return jnp.concatenate(tiles, axis=1)
 
 
-def as_column(row, size):
-    shape = (size, row.shape[1])
-    return jnp.sum(jnp.where(iota(shape, 0) == iota(shape, 1), row, 0.0), axis=1, keepdims=True)
-
-
-def split(x):
-    high = x.astype(BF16)
-    return high, (x - high.astype(F32)).astype(BF16)
-
-
-def pooling_table():
-    core = np.zeros((2, 128, 3, 128), np.float32)
-    side = np.zeros((128, 5, 3, 128), np.float32)
-
-    def add(pair, dx, lane, section, coarse, left, right):
-        for fine in (2 * coarse, 2 * coarse + 1):
-            if left and -2 <= fine <= 3:
-                side[16 * section + fine + 2, pair, dx, lane] = 0.25
-            elif right and 124 <= fine <= 129:
-                side[16 * section + 10 + fine - 124, pair, dx, lane] = 0.25
-            elif not left and not right:
-                core[section % 2, fine, dx, lane] = 0.25
-
-    for section in range(8):
-        for dx in range(3):
-            for m in range(64):
-                at = m + dx - 1
-                add(section // 2, dx, 64 * (section % 2) + m, section, at, at < 0, at > 63)
-            for n, m in enumerate((0, 1, 62, 63)):
-                add(4, dx, 4 * section + n, section, m + dx - 1, n < 2, n >= 2)
-    core = np.concatenate([np.concatenate([core[n], core[n]]) for n in range(2)]).reshape(512, 384)
-    side = np.concatenate([side, side]).reshape(256, 5 * 384)
-    return core.astype(ml_dtypes.bfloat16), side.astype(ml_dtypes.bfloat16)
-
-
-def network_kernel(
-    place,
-    order_ref,
-    margins_ref,
-    b_o_ref,
-    got_ref,
+def prepare(
+    pad_ref,
     w_in_ref,
     b_in_ref,
     w_a_ref,
@@ -195,21 +61,14 @@
     b_d_ref,
     w_u_ref,
     w_o_ref,
-    pool_core_ref,
-    pool_side_ref,
-    out_ref,
-    pad_ref,
+    b_o_ref,
     conv_in_ref,
     conv_a_ref,
     conv_d_ref,
-    raw_ref,
-    h_ref,
-    a_ref,
-    d_ref,
-    e_ref,
+    w_q_ref,
+    w_s_ref,
+    bias_ref,
 ):
-    gi, gj = place()
-
     pad_ref[...] = jnp.zeros_like(pad_ref)
     pad_ref[0:27, 0:28, 0:28] = w_a_ref[...]
     lane = iota((32, 512), 1)
@@ -249,9 +108,9 @@
             moved = jnp.where(within(lane, 384, 575), pltpu.roll(taps, 288, 1), 0.0) + jnp.where(
                 lane >= 672, pltpu.roll(taps, 672, 1), 0.0
             )
-        conv_d_ref[40 * n : 40 * n + 40] = moved
-    bias_a = as_column(b_a_ref[...], 32)
-    bias_d = jnp.concatenate([as_column(b_d_ref[...], 40)] * 8, axis=0)
+        conv_d_ref[40 * n : 40 * n + 40] = moved.astype(BF16)
+    bias_ref[0:32] = jnp.broadcast_to(as_column(b_a_ref[...], 32), (32, 128))
+    bias_ref[32:72] = jnp.broadcast_to(as_column(b_d_ref[...], 40), (40, 128))
 
     pad_ref[0] = jnp.zeros((32, 128), BF16)
     pad_ref[0, 0:9, 0:28] = w_in_ref[...]
@@ -290,26 +149,238 @@
     w_u = w_u + pltpu.roll(w_u, 80, 1)
     w_q = dot(w_o.astype(BF16), w_u.astype(BF16))
     lane = iota((24, 256), 1)
-    w_q = jnp.where(lane // 40 == (iota((24, 256), 0) % 8) // 2, w_q, 0.0)[:, 0:160]
-    w_q_high, w_q_low = split(w_q)
-    w_q = jnp.concatenate([w_q_high.astype(F32), w_q_low.astype(F32)], axis=0).astype(BF16)
+    w_q = jnp.where(lane // 40 == (iota((24, 256), 0) % 8) // 2, w_q, 0.0)
+    high = w_q.astype(BF16).astype(F32)
+    w_q_ref[...] = jnp.concatenate([high, w_q - high], axis=0).astype(BF16)
     w_o = jnp.concatenate([w_o] * 12, axis=1)
     w_o = jnp.concatenate([w_o, w_o], axis=0)
     lane = iota((48, 384), 1) // 32
     row = iota((48, 384), 0)
     block = jnp.where(row < 24, row % 8, jnp.where(within(row % 8, 3, 4), row % 8 + 5, row % 8))
-    w_o = jnp.where(lane == block, w_o, 0.0).astype(BF16)[:, 0:320]
-    row = iota((48, 1), 0) % 24
-    bias_o = jnp.where(row < 8, b_o_ref[0], jnp.where(row < 16, b_o_ref[1], b_o_ref[2]))
-
-    row = iota((256, 256), 0) % 128
-    spread = (row == iota((256, 256), 1) // 2).astype(F32).astype(BF16)
-    row = iota((256, 128), 0) % 128
-    lane = iota((256, 128), 1)
-    which = jnp.where(
-        within(lane % 16, 2, 5), lane % 16 // 2 - 1, jnp.where(within(lane % 16, 10, 13), lane % 16 // 2 - 3, -999)
+    w_s_ref[...] = jnp.where(lane == block, w_o, 0.0).astype(BF16)
+    row = iota((48, 128), 0) % 24
+    bias_ref[72:120] = jnp.where(row < 8, b_o_ref[0], jnp.where(row < 16, b_o_ref[1], b_o_ref[2]))
+    bias_ref[120:128] = jnp.zeros((8, 128), F32)
+
+
+def exchange_kernel(*refs):
+    raw_hbm, hbm, b_o_ref = refs[0], refs[1:9], refs[9]
+    got_ref, made = refs[10], refs[11:17]
+    raw_ref, vmem, pad_ref, send_ref = refs[17], refs[18:26], refs[26], refs[27]
+    raw_sem, load_sem, send_sem, recv_sem = refs[28:32]
+    gi = lax.axis_index("gx")
+    gj = lax.axis_index("gy")
+    odd, column, beside = neighbours(gi)
+    load_raw = pltpu.make_async_copy(raw_hbm, raw_ref, raw_sem)
+    load_raw.start()
+    loads = [pltpu.make_async_copy(hbm[n], vmem[n], load_sem.at[n]) for n in range(8)]
+    for load in loads:
+        load.start()
+    barrier = pltpu.get_barrier_semaphore()
+
+    def greet(n, carry):
+        strip = lax.rem(2 * gj + 15 + lax.rem(n, 4), 16)
+        slab = lax.div(n, 4)
+
+        @pl.when((strip != gi) | (slab != gj))
+        def _():
+            pl.semaphore_signal(barrier, inc=1, device_id=(strip, slab), device_id_type=MESH)
+
+        return carry
+
+    lax.fori_loop(0, 32, greet, 0)
+
+    lane = iota((128, 256), 1)
+    wanted = iota((128, 256), 0) + jnp.where(lane < 128, -4, 4)
+    rows = (wanted == lane % 128).astype(F32).astype(BF16)
+    load_raw.wait()
+    raw = raw_ref[0].astype(F32)
+    none = jnp.zeros_like(raw)
+    raw = jnp.concatenate(
+        [jnp.concatenate([raw, none], axis=1), jnp.concatenate([none, raw], axis=1)], axis=0
+    ).astype(BF16)
+    message = lax.dot_general(
+        rows, raw, (((1,), (1,)), ((), ())), preferred_element_type=F32
+    ).astype(BF16)
+    lane = iota((128, 128), 1)
+    even = jnp.where(within(lane, 6, 9), lane - 6, jnp.where(within(lane, 22, 25), lane + 42, -1))
+    uneven = jnp.where(
+        within(lane, 118, 121), lane - 58, jnp.where(within(lane, 102, 105), lane + 22, -1)
     )
-    spread_side = (row == 4 * (lane // 16) + which).astype(F32).astype(BF16)
+    cols = jnp.where((gi == 0) | (gi == 15), -1, jnp.where(odd == 1, uneven, even))
+    cols = (iota((128, 128), 0) == cols).astype(F32).astype(BF16)
+    send_ref[0:16] = message.reshape(16, 8, 128)
+    send_ref[16:32] = dot(message, cols).astype(BF16).reshape(16, 8, 128)
+
+    at_home = (gj == column) | (gj == beside)
+
+    @pl.when(at_home)
+    def _():
+        pl.semaphore_wait(barrier, 31)
+
+    @pl.when(jnp.logical_not(at_home))
+    def _():
+        pl.semaphore_wait(barrier, 32)
+
+    def send(n, carry):
+        target = lax.rem(gi + n, 16)
+        for kind in range(2):
+            where_to = column if kind == 0 else beside
+            slot = odd if kind == 0 else 3 - odd
+            source = send_ref.at[target + 16 * kind]
+            place = got_ref.at[slot, gj]
+            here = (target == gi) & (where_to == gj)
+
+            @pl.when(here)
+            def _():
+                pltpu.make_async_copy(source, place, recv_sem).start()
+
+            @pl.when(jnp.logical_not(here))
+            def _():
+                pltpu.make_async_remote_copy(
+                    src_ref=source,
+                    dst_ref=place,
+                    send_sem=send_sem,
+                    recv_sem=recv_sem,
+                    device_id=(target, where_to),
+                    device_id_type=MESH,
+                ).start()
+
+        return carry
+
+    lax.fori_loop(0, 16, send, 0)
+    for load in loads:
+        load.wait()
+    prepare(pad_ref, *vmem, b_o_ref, *made)
+    pltpu.make_async_copy(got_ref, got_ref, recv_sem).wait()
+
+    @pl.when(at_home)
+    def _():
+        pltpu.make_async_copy(send_ref.at[0:31], send_ref.at[0:31], send_sem).wait()
+
+    @pl.when(jnp.logical_not(at_home))
+    def _():
+        pltpu.make_async_copy(send_ref, send_ref, send_sem).wait()
+
+
+MADE = (
+    jax.ShapeDtypeStruct((448, 128), BF16),
+    jax.ShapeDtypeStruct((480, 512), BF16),
+    jax.ShapeDtypeStruct((320, 768), BF16),
+    jax.ShapeDtypeStruct((48, 256), BF16),
+    jax.ShapeDtypeStruct((48, 384), BF16),
+    jax.ShapeDtypeStruct((128, 128), F32),
+)
+
+
+def as_they_lie(raw, w_in, b_in, w_a, b_a, w_d, b_d, w_u, w_o):
+    return (
+        jnp.transpose(raw, (0, 2, 1)),
+        w_in.T,
+        b_in[None],
+        w_a,
+        b_a[None],
+        jnp.transpose(w_d, (0, 2, 1)),
+        b_d[None],
+        w_u,
+        w_o,
+    )
+
+
+def exchange(b_o, *arrays):
+    arrays = as_they_lie(*arrays)
+    vmem = pl.BlockSpec(memory_space=pltpu.VMEM)
+    return pl.pallas_call(
+        exchange_kernel,
+        out_shape=(jax.ShapeDtypeStruct((4, 8, 8, 128), BF16),) + MADE,
+        in_specs=[pl.BlockSpec(memory_space=pltpu.HBM)] * 9
+        + [pl.BlockSpec(memory_space=pltpu.SMEM)],
+        out_specs=(pl.BlockSpec(memory_space=pl.ANY),) + (vmem,) * 6,
+        scratch_shapes=[pltpu.VMEM(x.shape, x.dtype) for x in arrays]
+        + [
+            pltpu.VMEM((27, 32, 128), BF16),
+            pltpu.VMEM((32, 8, 128), BF16),
+            pltpu.SemaphoreType.DMA,
+            pltpu.SemaphoreType.DMA((8,)),
+            pltpu.SemaphoreType.DMA,
+            pltpu.SemaphoreType.DMA,
+        ],
+        compiler_params=pltpu.CompilerParams(
+            collective_id=0, has_side_effects=True, vmem_limit_bytes=12 * 1024 * 1024
+        ),
+    )(*arrays, b_o)
+
+
+def tables():
+    pool = np.zeros((768, 128), np.float32)
+    shift = np.zeros((5, 256, 256), np.float32)
+    spread = np.zeros((256, 256), np.float32)
+    spread_side = np.zeros((256, 128), np.float32)
+    for row in range(2):
+        for section in range(2):
+            for x in range(128):
+                pool[256 * section + 128 * row + x, 64 * section + x // 2] = 0.25
+        for section in range(8):
+            for x in range(6):
+                pool[512 + 128 * row + 16 * section + x, 8 * section + x // 2] = 0.25
+                pool[512 + 128 * row + 16 * section + 10 + x, 8 * section + 4 + x // 2] = 0.25
+        for lane in range(256):
+            spread[128 * row + lane // 2, lane] = 1
+        for section in range(8):
+            for x in range(4):
+                at = 128 * row + 8 * section
+                spread_side[at + 1 + x // 2, 16 * section + 2 + x] = 1
+                spread_side[at + 4 + x // 2, 16 * section + 10 + x] = 1
+    for section in range(8):
+        for m in range(64):
+            lane = 64 * (section % 2) + m
+            for side, step in ((0, -1), (1, 1)):
+                at = m + step
+                if at < 0:
+                    source = 128 + 8 * section
+                elif at > 63:
+                    source = 128 + 8 * section + 6
+                else:
+                    source = lane + step
+                shift[section // 2, source, 128 * side + lane] = 1
+        for lane, before, beyond in ((1, 0, 2), (2, 1, None), (4, None, 5), (5, 4, 6)):
+            for side, source in ((0, before), (1, beyond)):
+                if source is not None:
+                    shift[4, 8 * section + source, 128 * side + 8 * section + lane] = 1
+    wide = np.concatenate([shift.reshape(1280, 256), spread])
+    narrow = np.concatenate([pool, spread_side])
+    return wide.astype(ml_dtypes.bfloat16), narrow.astype(ml_dtypes.bfloat16)
+
+
+def network_kernel(
+    place,
+    order_ref,
+    margins_ref,
+    got_ref,
+    conv_in_ref,
+    conv_a_ref,
+    conv_d_ref,
+    w_q_ref,
+    w_s_ref,
+    bias_ref,
+    wide_hbm,
+    narrow_hbm,
+    out_ref,
+    wide_ref,
+    narrow_ref,
+    raw_ref,
+    h_ref,
+    a_ref,
+    d_ref,
+    e_ref,
+    wide_sem,
+    narrow_sem,
+):
+    gi, gj = place()
+    load_wide = pltpu.make_async_copy(wide_hbm, wide_ref, wide_sem)
+    load_narrow = pltpu.make_async_copy(narrow_hbm, narrow_ref, narrow_sem)
+    load_narrow.start()
+    load_wide.start()
 
     def margin(step_y, step_x):
         y, x = gi + step_y, gj + step_x
@@ -359,9 +430,17 @@
         for k in range(8):
             slab = slab + jnp.where(order_ref[k] == z, k, 0)
         near, far, before, after = [got_ref[n, slab].astype(F32) for n in range(4)]
-        core = jnp.where(tile < 64, near, far)
-        low = jnp.where(tile < 6, far, after)
-        high = jnp.where(tile >= 122, near, before)
+        core = jnp.concatenate(
+            [
+                jnp.where(lane < 64, near, pltpu.roll(far, 64, 1)),
+                jnp.where(lane < 64, pltpu.roll(near, 64, 1), far),
+            ],
+            axis=0,
+        )
+        before = jnp.concatenate([before, pltpu.roll(before, 16, 1)], axis=0)
+        after = jnp.concatenate([after, pltpu.roll(after, 112, 1)], axis=0)
+        low = jnp.where(tile < 6, pltpu.roll(core, 6, 1), after)
+        high = jnp.where(tile >= 122, pltpu.roll(core, 122, 1), before)
         beside = jnp.where(tile < 64, low, high)
         for n in range(5):
             s = n - 2
@@ -402,6 +481,8 @@
             )
             h = jnp.maximum(dot(conv_in_ref[:, 0:64], taps).astype(BF16), 0)
             h_ref[:, dx, :, at] = h.reshape(14, 32, h.shape[1])
+
+    bias_a = bias_ref[0:32]
 
     def residual(three):
         extra = three in (1, 2)
@@ -450,26 +531,37 @@
         late = jnp.concatenate([a_ref[n, :, at] for n in (1, 3, 5, 7, 9, 13, 10, 7)], axis=0)
         return jnp.concatenate([even, late], axis=1)
 
-    side = pooled_rows(slice(1024, 1152))
+    load_narrow.wait()
+    load_wide.wait()
+
+    def store(dx, at, value):
+        d_ref[:, dx, :, at] = value.reshape(8, 32, 128)
+
+    margins = dot(pooled_rows(slice(1024, 1152)), narrow_ref[512:768]).astype(BF16)
     for q in range(5):
-        d = dot(side, pool_side_ref[:, 384 * q : 384 * q + 384])
+        at = slice(128 * q, 128 * q + 128)
         if q < 4:
-            for half in range(2):
-                z = 2 * q + half
-                core = pooled_rows(slice(128 * z, 128 * z + 128))
-                d = d + dot(core, pool_core_ref[256 * half : 256 * half + 256])
-        for dx in range(3):
-            part = d[:, 128 * dx : 128 * dx + 128].astype(BF16)
-            d_ref[:, dx, :, 128 * q : 128 * q + 128] = part.reshape(8, 32, 128)
-
-    conv_d = conv_d_ref[...].astype(BF16)
+            both = [pooled_rows(slice(128 * z, 128 * z + 128)) for z in (2 * q, 2 * q + 1)]
+            d = dot(jnp.concatenate(both, axis=1), narrow_ref[0:512]).astype(BF16)
+            moved = dot(
+                jnp.concatenate([d, margins], axis=1), wide_ref[256 * q : 256 * q + 256]
+            ).astype(BF16)
+        else:
+            d = margins
+            moved = dot(d, wide_ref[1024:1152]).astype(BF16)
+        store(1, at, d)
+        store(0, at, moved[:, 0:128])
+        store(2, at, moved[:, 128:256])
+
+    bias_d = jnp.concatenate([bias_ref[32:72]] * 8, axis=0)
     for at in (slice(0, 256), slice(256, 512), slice(512, 640)):
-        e = dot(conv_d, d_ref[:, :, :, at].reshape(768, at.stop - at.start))
-        e_ref[:, at] = jnp.maximum(e + bias_d, 0.0).astype(BF16)
+        e = dot(conv_d_ref[...], d_ref[:, :, :, at].reshape(768, at.stop - at.start))
+        e = e + (bias_d if e.shape[1] == 128 else jnp.concatenate([bias_d, bias_d], axis=1))
+        e_ref[:, at] = jnp.maximum(e, 0.0).astype(BF16)
 
     lifted = []
     for kind in range(2):
-        q = dot(w_q, e_ref[160 * kind : 160 * kind + 160])
+        q = dot(w_q_ref[:, 0:160], e_ref[160 * kind : 160 * kind + 160])
         lifted.append(q[0:24] + q[24:48])
     q = jnp.concatenate(lifted, axis=0)
     high = q.astype(BF16).astype(F32)
@@ -479,16 +571,19 @@
         at = slice(128 * n, 128 * n + 128)
         return jnp.concatenate([high[:, at], low[:, at]], axis=1).astype(BF16)
 
+    bias_o = bias_ref[72:120]
+
     def logits(at):
-        return dot(w_o, a_ref[2:12, :, at].reshape(320, at.stop - at.start)) + bias_o
+        s = dot(w_s_ref[:, 0:320], a_ref[2:12, :, at].reshape(320, at.stop - at.start))
+        return s + (bias_o if s.shape[1] == 128 else jnp.concatenate([bias_o, bias_o], axis=1))
 
     at = slice(1024, 1152)
-    beyond = jax.nn.sigmoid(logits(at) + dot(both(4), spread_side))
+    beyond = jax.nn.sigmoid(logits(at) + dot(both(4), narrow_ref[768:1024]))
     beyond = [
         beyond[8 * o : 8 * o + 8] * weight_x + beyond[24 + 8 * o : 32 + 8 * o] * weight_xy
         for o in range(3)
     ]
-    up = dot(jnp.concatenate([both(n) for n in range(4)], axis=0), spread)
+    up = dot(jnp.concatenate([both(n) for n in range(4)], axis=0), wide_ref[1280:1536])
     for n in range(4):
         at = slice(256 * n, 256 * n + 256)
         s = jax.nn.sigmoid(logits(at) + up[48 * n : 48 * n + 48])
@@ -500,42 +595,29 @@
                 out_ref[o, z] = fold(own + other * weight_y, beyond[o], z) * scale
 
 
-def network(place, order, margins, b_o, got, w_in, b_in, w_a, b_a, w_d, b_d, w_u, w_o, **options):
+def network(place, order, margins, got, *made, **options):
     smem = pl.BlockSpec(memory_space=pltpu.SMEM)
     vmem = pl.BlockSpec(memory_space=pltpu.VMEM)
+    hbm = pl.BlockSpec(memory_space=pltpu.HBM)
     return pl.pallas_call(
         functools.partial(network_kernel, place),
         out_shape=jax.ShapeDtypeStruct((3, 8, 8, 128), F32),
-        in_specs=[smem] * 3 + [vmem] * 11,
+        in_specs=[smem] * 2 + [vmem] * 7 + [hbm] * 2,
         out_specs=vmem,
         scratch_shapes=[
-            pltpu.VMEM((27, 32, 128), BF16),
-            pltpu.VMEM((448, 128), BF16),
-            pltpu.VMEM((480, 512), BF16),
-            pltpu.VMEM((320, 768), F32),
+            pltpu.VMEM((1536, 256), BF16),
+            pltpu.VMEM((1024, 128), BF16),
             pltpu.VMEM((80, 1152), BF16),
             pltpu.VMEM((14, 3, 32, 1152), BF16),
             pltpu.VMEM((14, 32, 1152), BF16),
             pltpu.VMEM((8, 3, 32, 640), BF16),
             pltpu.VMEM((320, 640), BF16),
+            pltpu.SemaphoreType.DMA,
+            pltpu.SemaphoreType.DMA,
         ],
-        compiler_params=pltpu.CompilerParams(vmem_limit_bytes=48 * 1024 * 1024),
+        compiler_params=pltpu.CompilerParams(vmem_limit_bytes=32 * 1024 * 1024),
         **options,
-    )(
-        order,
-        margins.T,
-        b_o,
-        got,
-        w_in.T,
-        b_in[None],
-        w_a,
-        b_a[None],
-        jnp.transpose(w_d, (0, 2, 1)),
-        b_d[None],
-        w_u,
-        w_o,
-        *pooling_table(),
-    )
+    )(order, margins.T, got, *made, *tables())
 
 
 def whereabouts():
@@ -543,10 +625,8 @@
 
 
 def per_device(raw, section_order, margins, w_in, b_in, w_a, b_a, w_d, b_d, w_u, w_o, b_o):
-    got = exchange(raw)
-    return network(
-        whereabouts, section_order, margins, b_o, got, w_in, b_in, w_a, b_a, w_d, b_d, w_u, w_o
-    )
+    got, *made = exchange(b_o, raw, w_in, b_in, w_a, b_a, w_d, b_d, w_u, w_o)
+    return network(whereabouts, section_order, margins, got, *made)
 
 
 def solution(mesh):

time: 29.7 us -> 32.7 us (1.10)
  local copies, waits for them, and re-layouts: 4.07 us -> 9.06 us
  Pallas kernels: 25.2 us -> 23.1 us
    unnamed x28, local copies, waits for them, and re-layouts: 4.07 us -> 9.06 us
    pallas_call x1, Pallas kernels: 18.8 us -> 16.6 us  [exchange(): pl.pallas_call(exchange_kernel, out_shape=(jax.ShapeDtypeStruct((4, 8, 8,...]
where the time goes in v2:
time: 32.7 us; the launch traced here: 32.2 us
  Pallas kernels  23.1 us (71%)
  local copies, waits for them, and re-layouts  9.06 us (28%)
    pallas_call x1, Pallas kernels, exchange(): pl.pallas_call(exchange_kernel, out_shape=(jax.ShapeDtypeStruct((4, 8, 8,...  16.6 us
    unnamed x28, local copies, waits for them, and re-layouts  9.06 us
    pallas_call x1, Pallas kernels, network(): pl.pallas_call(functools.partial(network_kernel, place), out_shape=jax.Sh...  6.57 us

profile of v2, /device:TPU:1, one launch (start us, length us, event | category | flops | bytes accessed | tf_op | source)
XLA Modules:
  0.0 32.2 jit_solution(2411601205130943284)
XLA Ops:
  0.0 0.0 copy-start.1
  0.0 0.0 copy-start.2
  0.0 1.0 %copy-done.2 = bf16[27,28,28]{2,1,0:T(8,128)(2,1)S(1)} copy-done((bf16[27,28,28]{2,1,0:T(8,128)(2,1)S(1)}, bf16[27,28,28]{2,1,0:T(8,128)(2,1)}, u32[]{:S(2)}) %copy-start.2) | copy-done | bytes 42360
  1.0 0.0 copy-start.3
  1.0 0.9 %copy-done.3 = bf16[9,36,28]{1,2,0:T(8,128)(2,1)S(1)} copy-done((bf16[9,36,28]{1,2,0:T(8,128)(2,1)S(1)}, bf16[9,36,28]{1,2,0:T(8,128)(2,1)}, u32[]{:S(2)}) %copy-start.3) | copy-done | bytes 18168
  1.9 0.0 copy-start.4
  1.9 0.7 %copy-done.4 = bf16[1,128,64]{1,2,0:T(8,128)(2,1)S(1)} copy-done((bf16[1,128,64]{1,2,0:T(8,128)(2,1)S(1)}, bf16[1,128,64]{1,2,0:T(8,128)(2,1)}, u32[]{:S(2)}) %copy-start.4) | copy-done | bytes 16408
  2.6 0.0 copy-start.5
  2.6 0.7 %copy-done.5 = bf16[28,36]{1,0:T(8,128)(2,1)S(1)} copy-done((bf16[28,36]{1,0:T(8,128)(2,1)S(1)}, bf16[28,36]{1,0:T(8,128)(2,1)}, u32[]{:S(2)}) %copy-start.5) | copy-done | bytes 2040
  3.3 0.0 copy-start.6
  3.3 0.7 %copy-done.6 = bf16[28,9]{0,1:T(8,128)(2,1)S(1)} copy-done((bf16[28,9]{0,1:T(8,128)(2,1)S(1)}, bf16[28,9]{0,1:T(8,128)(2,1)}, u32[]{:S(2)}) %copy-start.6) | copy-done | bytes 528
  4.0 0.0 copy-start.8
  4.0 0.7 %copy-done.8 = bf16[3,28]{1,0:T(4,128)(2,1)S(1)} copy-done((bf16[3,28]{1,0:T(4,128)(2,1)S(1)}, bf16[3,28]{1,0:T(4,128)(2,1)}, u32[]{:S(2)}) %copy-start.8) | copy-done | bytes 192
  4.6 0.0 copy-start.9
  4.7 0.7 %copy-done.9 = f32[28]{0:T(128)S(1)} copy-done((f32[28]{0:T(128)S(1)}, f32[28]{0:T(128)}, u32[]{:S(2)}) %copy-start.9) | copy-done | bytes 136
  5.3 0.0 copy-start.10
  5.3 0.7 %copy-done.10 = f32[28]{0:T(128)S(1)} copy-done((f32[28]{0:T(128)S(1)}, f32[28]{0:T(128)}, u32[]{:S(2)}) %copy-start.10) | copy-done | bytes 136
  6.0 0.0 copy-start.11
  6.0 0.7 %copy-done.11 = f32[36]{0:T(128)S(1)} copy-done((f32[36]{0:T(128)S(1)}, f32[36]{0:T(128)}, u32[]{:S(2)}) %copy-start.11) | copy-done | bytes 168
  6.6 0.0 copy-start.12
  6.6 0.7 %copy-done.12 = f32[3]{0:T(128)S(1)} copy-done((f32[3]{0:T(128)S(1)}, f32[3]{0:T(128)}, u32[]{:S(2)}) %copy-start.12) | copy-done | bytes 36
  7.3 16.6 %shard_map.136 = (bf16[4,8,8,128]{3,2,1,0:T(8,128)(2,1)S(1)}, bf16[448,128]{1,0:T(8,128)(2,1)S(1)}, bf16[480,512]{1,0:T(8,128)(2,1)S(1)}, bf16[320,768]{1,0:T(8,...) custom-call(bf16[1,64,128]{2,1,0:T(8,128)(2,1)S(1)} %bitcast.8, ...), custom_call_target="tpu_custom_call" | custom-call | tf_op jit(solution)/shard_map/pallas_call | solution.py:293
  23.8 0.0 copy-start.7
  23.8 0.0 copy-start.13
  23.9 0.0 copy-done.1
  23.9 0.7 %copy-done.7 = s32[16,8]{0,1:T(8,128)S(1)} copy-done((s32[16,8]{0,1:T(8,128)S(1)}, s32[16,8]{0,1:T(8,128)}, u32[]{:S(2)}) %copy-start.7) | copy-done | bytes 536
  24.5 0.0 copy-done.13
  24.5 0.0 copy-start
  24.5 1.1 %copy-done = bf16[1536,256]{1,0:T(8,128)(2,1)S(1)} copy-done((bf16[1536,256]{1,0:T(8,128)(2,1)S(1)}, bf16[1536,256]{1,0:T(8,128)(2,1)}, u32[]{:S(2)}) %copy-start) | copy-done | bytes 786456
  25.7 6.6 %shard_map.137 = f32[3,8,8,128]{3,2,1,0:T(8,128)} custom-call(s32[8]{0:T(128)S(1)} %copy-done.13, s32[8,16]{1,0:T(8,128)S(1)} %bitcast.10, bf16[4,8,8,128]{3,2,1,0:T(8,128)(2,1)S(1)} %get-tuple-element.12.got_ref, bf16[448,128]{1,0:T(8,128)(2,1)S(1)} %get-tuple-element.13.conv_in_ref, bf16[480,512]{1,0:T(8,128)(2,1)S(1)} %get-tuple-element.14.conv_a_ref, ...), custom_call_target="tpu_custom_call" | custom-call | tf_op jit(solution)/shard_map/pallas_call | solution.py:602
Async XLA Ops:
  0.0 23.9 %copy-start.1 = (bf16[1024,128]{1,0:T(8,128)(2,1)S(1)}, bf16[1024,128]{1,0:T(8,128)(2,1)}, u32[]{:S(2)}) copy-start(bf16[1024,128]{1,0:T(8,128)(2,1)} %constant.5.clone.narrow_hbm) | copy-start | bytes 786436
  0.0 1.0 %copy-start.2 = (bf16[27,28,28]{2,1,0:T(8,128)(2,1)S(1)}, bf16[27,28,28]{2,1,0:T(8,128)(2,1)}, u32[]{:S(2)}) copy-start(bf16[27,28,28]{2,1,0:T(8,128)(2,1)} %refs_3_.1) | copy-start | bytes 127012
  1.0 0.9 %copy-start.3 = (bf16[9,36,28]{1,2,0:T(8,128)(2,1)S(1)}, bf16[9,36,28]{1,2,0:T(8,128)(2,1)}, u32[]{:S(2)}) copy-start(bf16[9,36,28]{1,2,0:T(8,128)(2,1)} %param.21) | copy-start | bytes 54436
  1.9 0.7 %copy-start.4 = (bf16[1,128,64]{1,2,0:T(8,128)(2,1)S(1)}, bf16[1,128,64]{1,2,0:T(8,128)(2,1)}, u32[]{:S(2)}) copy-start(bf16[1,128,64]{1,2,0:T(8,128)(2,1)} %param.14) | copy-start | bytes 49156
  2.6 0.7 %copy-start.5 = (bf16[28,36]{1,0:T(8,128)(2,1)S(1)}, bf16[28,36]{1,0:T(8,128)(2,1)}, u32[]{:S(2)}) copy-start(bf16[28,36]{1,0:T(8,128)(2,1)} %refs_7_.1) | copy-start | bytes 6052
  3.3 0.7 %copy-start.6 = (bf16[28,9]{0,1:T(8,128)(2,1)S(1)}, bf16[28,9]{0,1:T(8,128)(2,1)}, u32[]{:S(2)}) copy-start(bf16[28,9]{0,1:T(8,128)(2,1)} %param.17) | copy-start | bytes 1516
  4.0 0.7 %copy-start.8 = (bf16[3,28]{1,0:T(4,128)(2,1)S(1)}, bf16[3,28]{1,0:T(4,128)(2,1)}, u32[]{:S(2)}) copy-start(bf16[3,28]{1,0:T(4,128)(2,1)} %refs_8_.1) | copy-start | bytes 508
  4.6 0.7 %copy-start.9 = (f32[28]{0:T(128)S(1)}, f32[28]{0:T(128)}, u32[]{:S(2)}) copy-start(f32[28]{0:T(128)} %param.18) | copy-start | bytes 340
  5.3 0.7 %copy-start.10 = (f32[28]{0:T(128)S(1)}, f32[28]{0:T(128)}, u32[]{:S(2)}) copy-start(f32[28]{0:T(128)} %param.20) | copy-start | bytes 340
  6.0 0.7 %copy-start.11 = (f32[36]{0:T(128)S(1)}, f32[36]{0:T(128)}, u32[]{:S(2)}) copy-start(f32[36]{0:T(128)} %param.22) | copy-start | bytes 436
  6.6 0.7 %copy-start.12 = (f32[3]{0:T(128)S(1)}, f32[3]{0:T(128)}, u32[]{:S(2)}) copy-start(f32[3]{0:T(128)} %refs_9_.1) | copy-start | bytes 40
  23.8 0.7 %copy-start.7 = (s32[16,8]{0,1:T(8,128)S(1)}, s32[16,8]{0,1:T(8,128)}, u32[]{:S(2)}) copy-start(s32[16,8]{0,1:T(8,128)} %param.16) | copy-start | bytes 1540
  23.8 0.7 %copy-start.13 = (s32[8]{0:T(128)S(1)}, s32[8]{0:T(128)}, u32[]{:S(2)}) copy-start(s32[8]{0:T(128)} %order_ref.1) | copy-start | bytes 100
  24.5 1.1 %copy-start = (bf16[1536,256]{1,0:T(8,128)(2,1)S(1)}, bf16[1536,256]{1,0:T(8,128)(2,1)}, u32[]{:S(2)}) copy-start(bf16[1536,256]{1,0:T(8,128)(2,1)} %constant.4.clone.wide_hbm) | copy-start | bytes 2359300
